TPU v7x, 128 devices: a whole 4x4x4 slice. The times are simulated.
128 devices in a mesh: group: 16 (over x, y), mp: 8 (over z, core).
Axes of the slice: x: 4, y: 4, z: 4, core: 2. Of those that a mesh axis runs over, the one named last changes fastest.
Arguments:
- node_features: bfloat16 [768, 262144], P('mp', 'group'), may hold values from -6 to 6
- target_nodes: int32 [16, 256], replicated, may hold values from 0 to 262143
- first_hop: int32 [16, 25, 256], replicated, may hold values from 0 to 262143
- live_counts: int32 [16], P('group'), may hold values from 64 to 256, as said below
- seed_links: int32 [16, 32, 15], P('group'), may hold values from 0 to 255, as said below
- seed_labels: int32 [16, 32], P('group'), may hold values from 0 to 152
- self_weight: bfloat16 [768, 1024], P('mp'), may hold values from -0.21875 to 0.21875
- neigh_weight: bfloat16 [768, 1024], P('mp'), may hold values from -0.21875 to 0.21875
- hidden_bias: float32 [1024], P('mp'), may hold values from -3 to 3
- class_self: bfloat16 [1024, 153], P('mp'), may hold values from -0.1875 to 0.1875
- class_neigh: bfloat16 [1024, 153], P('mp'), may hold values from -0.1875 to 0.1875
- class_bias: float32 [153], replicated, may hold values from -4 to 4
Outputs:
- hidden_layer: bfloat16 [4096, 1024], P('group', 'mp')
- grad_self: float32 [768, 1024], P('mp')
- grad_neigh: float32 [768, 1024], P('mp')
- grad_hbias: float32 [1024], P('mp')
- grad_cself: float32 [1024, 153], P('mp')
- grad_cneigh: float32 [1024, 153], P('mp')
- grad_cbias: float32 [153], replicated
- mean_loss: float32 [], replicated
Inputs may be any that keep to these rules, and one draw needn't show every extreme that they name: live_counts[b] target slots of batch b are live; slots 0 to 31 are its seeds; slots at or beyond live_counts[b] are padding whose ids carry no meaning; some batch is full. seed_links[b, s, k] < live_counts[b].
All inputs are finite; a program needn't handle non-finite values.
Results may differ from a plain program's by a relative error of at most 0.0095.
Values sent between devices are 32-bit elements; how exact they have to be, the bound alone decides.
A program may use at most 128 MiB of HBM per device.

v0:
```python
import jax
import jax.numpy as jnp
from jax import lax
from jax.sharding import PartitionSpec as P


def body(
    node_features,
    target_nodes,
    first_hop,
    live_counts,
    seed_links,
    seed_labels,
    self_weight,
    neigh_weight,
    hidden_bias,
    class_self,
    class_neigh,
    class_bias,
):
    high = lax.Precision.HIGHEST
    feat_cols = node_features.shape[0]
    node_rows = node_features.shape[1]
    mp_count = lax.axis_size("mp")
    group_count = lax.axis_size("group")
    targets = target_nodes.shape[1]
    hid_cols = hidden_bias.shape[0]
    offset = lax.axis_index("group") * node_rows

    def local_cols(node_ids):
        local = node_ids - offset
        inside = (local >= 0) & (local < node_rows)
        cols = jnp.take(node_features, jnp.clip(local, 0, node_rows - 1), axis=1)
        return jnp.where(inside[None], cols.astype(jnp.float32), 0.0)

    self_part = local_cols(target_nodes)

    def add_slot(running, node_ids):
        return (running + local_cols(node_ids), None)

    neigh_total, _unused = lax.scan(
        add_slot, jnp.zeros_like(self_part), jnp.moveaxis(first_hop, 1, 0)
    )
    neigh_part = neigh_total / first_hop.shape[1]
    self_blocks = (
        self_weight.astype(jnp.float32).reshape(feat_cols, mp_count, hid_cols).transpose(1, 0, 2)
    )
    neigh_blocks = (
        neigh_weight.astype(jnp.float32).reshape(feat_cols, mp_count, hid_cols).transpose(1, 0, 2)
    )
    block_ids = jnp.arange(1 * lax.axis_size(("group", "mp")))
    owner = block_ids // mp_count
    column = block_ids % mp_count
    self_pick = jnp.take(self_part, owner, axis=1)
    neigh_pick = jnp.take(neigh_part, owner, axis=1)
    pre = lax.psum_scatter(
        jnp.einsum("fct,cfh->cth", self_pick, jnp.take(self_blocks, column, axis=0), precision=high)
        + jnp.einsum(
            "fct,cfh->cth", neigh_pick, jnp.take(neigh_blocks, column, axis=0), precision=high
        ),
        ("group", "mp"),
        scatter_dimension=0,
        tiled=True,
    )[0]
    pre = pre + hidden_bias
    live = jnp.arange(targets) < live_counts[0]
    hidden_layer = jnp.where(live[:, None], jnp.maximum(pre, 0.0), 0.0).astype(jnp.bfloat16)
    active = hidden_layer.astype(jnp.float32)
    seeds = seed_links.shape[1]
    fan_two = seed_links.shape[2]
    links = seed_links[0]
    adjacency = (
        jnp.sum(
            (links[:, :, None] == jnp.arange(targets)[None, None, :]).astype(jnp.float32), axis=1
        )
        / fan_two
    )
    seed_self = active[:seeds]
    seed_neigh = jnp.dot(adjacency, active, precision=high)
    cself = class_self.astype(jnp.float32)
    cneigh = class_neigh.astype(jnp.float32)
    partial_logits = jnp.dot(seed_self, cself, precision=high) + jnp.dot(
        seed_neigh, cneigh, precision=high
    )
    logits = lax.psum(partial_logits, "mp") + class_bias
    log_total = jnp.log(jnp.sum(jnp.exp(logits), axis=-1, keepdims=True))
    onehot = (seed_labels[0][:, None] == jnp.arange(logits.shape[1])[None, :]).astype(jnp.float32)
    losses = log_total[:, 0] - jnp.sum(onehot * logits, axis=-1)
    dlogit = jnp.exp(logits - log_total) - onehot
    back_self = jnp.dot(dlogit, cself.T, precision=high)
    back_neigh = jnp.dot(dlogit, cneigh.T, precision=high)
    grad_act = jnp.dot(adjacency.T, back_neigh, precision=high) + jnp.pad(
        back_self, ((0, targets - seeds), (0, 0))
    )
    grad_pre = jnp.where(live[:, None] & (pre > 0), grad_act, 0.0)
    piece = lax.all_gather(grad_pre[None], ("group", "mp"), axis=0, tiled=True)
    block_ids = jnp.arange(piece.shape[0])
    owner = block_ids // mp_count
    column = block_ids % mp_count
    select = (column[:, None] == jnp.arange(mp_count)[None, :]).astype(jnp.float32)
    self_pick = jnp.take(self_part, owner, axis=1)
    neigh_pick = jnp.take(neigh_part, owner, axis=1)
    self_term = jnp.einsum("fct,cth,cm->fmh", self_pick, piece, select, precision=high)
    neigh_term = jnp.einsum("fct,cth,cm->fmh", neigh_pick, piece, select, precision=high)
    weight_grads = jnp.stack([self_term, neigh_term]).reshape(2, feat_cols, mp_count * hid_cols)
    local_terms = (
        weight_grads,
        jnp.sum(grad_pre, axis=0),
        jnp.sum(losses),
        jnp.sum(dlogit, axis=0),
        jnp.dot(seed_self.T, dlogit, precision=high),
        jnp.dot(seed_neigh.T, dlogit, precision=high),
    )
    totals = lax.psum(
        (
            local_terms[0],
            local_terms[1],
            local_terms[2],
            local_terms[3],
            local_terms[4],
            local_terms[5],
        ),
        "group",
    )
    mean_loss = totals[2] / (group_count * seeds)
    return (
        hidden_layer,
        totals[0][0],
        totals[0][1],
        totals[1],
        totals[4],
        totals[5],
        totals[3],
        mean_loss,
    )


def solution(mesh):
    in_specs = (
        P("mp", "group"),
        P(),
        P(),
        P("group"),
        P("group", None, None),
        P("group", None),
        P("mp", None),
        P("mp", None),
        P("mp"),
        P("mp", None),
        P("mp", None),
        P(),
    )
    out_specs = (
        P("group", "mp"),
        P("mp", None),
        P("mp", None),
        P("mp"),
        P("mp", None),
        P("mp", None),
        P(),
        P(),
    )
    return jax.shard_map(body, mesh=mesh, in_specs=in_specs, out_specs=out_specs, check_vma=False)
```

profile of v0, /device:TPU:0, one launch (start us, length us, event | category | flops | bytes accessed | tf_op | source)
XLA Modules:
  0.0 1485.7 jit_solution(17615729459530361920)
XLA Ops:
  14.6 435.9 %while.11 = (s32[]{:T(128)}, f32[96,16,256]{0,2,1:T(8,128)S(1)}, s32[25,16,256]{2,1,0:T(8,128)}, s32[]{:T(128)}, bf16[96,16384]{0,1:T(8,128)(2,1)}, /*index=5*/s32[]{:T(128)}, s32[]{:T(128)}) while((s32[]{:T(128)}, f32[96,16,256]{0,2,1:T(8,128)S(1)}, s32[25,16,256]{2,1,0:T(8,128)}, s32[]{:T(128)}, bf16[96,16384]{0,1:T(8,128)(2,1)}, ...), condition=%wide.region_1.5_spmd.clone, body=%wide.region_0.4_spmd.clone.sunk | while | flops 2039811 | bytes 5668975 | solution.py:41
  15.4 13.8 gather_fusion
  32.9 13.8 gather_fusion
  50.3 13.8 gather_fusion
  137.5 13.8 gather_fusion
  224.7 13.8 gather_fusion
  242.1 13.8 gather_fusion
  259.5 13.8 gather_fusion
  277.0 13.8 gather_fusion
  329.3 13.8 gather_fusion
  346.7 13.8 gather_fusion
  364.2 13.8 gather_fusion
  416.5 13.8 gather_fusion
  433.9 13.8 gather_fusion
  453.8 16.9 %gather_fusion.1 = bf16[4096,96]{1,0:T(8,128)(2,1)} fusion(bf16[96,16384]{0,1:T(8,128)(2,1)} %get-tuple-element.171, s32[4096]{0:T(1024)S(1)} %broadcast_clamp_fusion.1), kind=kCustom, calls=%fused_computation.3.clone | custom fusion | bytes 1589248 | tf_op jit(solution)/shard_map/jit(_take)/gather | solution.py:33
  492.9 20.8 %fusion.3 = f32[128,256,128]{2,1,0:T(8,128)S(1)} fusion(f32[128,96,256]{1,2,0:T(8,128)} %gather_fusion.4, pred[128]{0:T(512)(128)(4,1)S(1)} %get-tuple-element.102, f32[128,96,128]{2,1,0:T(8,128)} %gather_fusion.5, pred[128]{0:T(512)(128)(4,1)S(1)} %get-tuple-element.101), kind=kOutput, calls=%fused_computation.15 | convolution fusion | flops 4836556800 | bytes 35651840 | tf_op jit(solution)/shard_map/fct,cfh->cth/dot_general | solution.py:58
  513.7 34.4 %fusion.13 = f32[128,256,128]{2,1,0:T(8,128)} fusion(f32[128,256,128]{2,1,0:T(8,128)S(1)} %fusion.3, f32[128,96,256]{2,1,0:T(8,128)} %gather_fusion.2, f32[128,96,128]{2,1,0:T(8,128)S(1)} %copy-done.2, pred[128]{0:T(512)(128)(4,1)S(1)} %get-tuple-element.102, pred[128]{0:T(512)(128)(4,1)S(1)} %get-tuple-element.101), kind=kOutput, calls=%fused_computation.25 | convolution fusion | flops 4840751104 | bytes 52429056 | tf_op jit(solution)/shard_map/fct,cfh->cth/dot_general | solution.py:57
  549.0 668.0 %reduce-scatter.2.cloned.1.call-done = f32[1,256,128]{2,1,0:T(8,128)} async-done(((f32[128,256,128]{2,1,0:T(8,128)}), f32[1,256,128]{2,1,0:T(8,128)}) %reduce-scatter.2.cloned.1.call-update) | async-done | bytes 131088 | tf_op jit(solution)/shard_map/reduce_scatter | solution.py:56
  1218.6 23.6 %psum.49 = f32[32,153]{1,0:T(8,128)S(1)} all-reduce(f32[32,153]{1,0:T(8,128)S(1)} %convolution_add_fusion.1), channel_id=1, replica_groups=mesh['group'=16,'mp'=8] {'mp'}, use_global_device_ids=true, to_apply=%region_4.8 | all-reduce | flops 4896 | bytes 39168 | tf_op jit(solution)/shard_map/psum | solution.py:85
  1246.9 73.3 %all-gather.3.cloned.1.call-done = f32[32768,128]{1,0:T(8,128)} async-done(((f32[256,128]{1,0:T(8,128)}), f32[32768,128]{1,0:T(8,128)}) %all-gather.3.cloned.1.call-update) | async-done | bytes 16777232 | tf_op jit(solution)/shard_map/all_gather | solution.py:96
  1320.2 19.8 %fusion.7 = f32[128,128,96]{1,2,0:T(8,128)} fusion(f32[128,256,128]{2,1,0:T(8,128)} %bitcast.97, f32[128,96,256]{2,1,0:T(8,128)} %gather_fusion.2, pred[128]{0:T(512)(128)(4,1)S(1)} %get-tuple-element.102), kind=kOutput, calls=%fused_computation.19 | convolution fusion | flops 4834983936 | bytes 35651712 | tf_op jit(solution)/shard_map/fct,cth,cm->fmh/dot_general | solution.py:103
  1340.0 32.5 %fusion.1 = f32[128,128,96]{1,2,0:T(8,128)} fusion(f32[128,256,128]{2,1,0:T(8,128)} %bitcast.98, f32[128,96,256]{1,2,0:T(8,128)} %gather_fusion.4, pred[128]{0:T(512)(128)(4,1)S(1)} %get-tuple-element.102), kind=kOutput, calls=%fused_computation.13 | convolution fusion | flops 4834983936 | bytes 35651712 | tf_op jit(solution)/shard_map/fct,cth,cm->fmh/dot_general | solution.py:104
  1387.7 41.1 %all-reduce.1 = (f32[128]{0:T(128)}, f32[153]{0:T(256)}, f32[]{:T(128)}) all-reduce(f32[128]{0:T(128)S(1)} %get-tuple-element.99, f32[153]{0:T(256)S(1)} %get-tuple-element.78, f32[]{:T(128)} %subtract_reduce_fusion), channel_id=1, replica_groups=mesh['group'=16,'mp'=8] {'group'}, use_global_device_ids=true, to_apply=%region_8.12 | all-reduce | flops 282 | bytes 2256 | tf_op jit(solution)/shard_map/psum | solution.py:114
  1429.5 43.4 %all-reduce.5.cloned.1.call-done = (f32[2,96,1024]{2,1,0:T(8,128)}, f32[128,153]{0,1:T(8,128)}, f32[128,153]{0,1:T(8,128)}) async-done(((f32[2,96,1024]{2,1,0:T(8,128)}, f32[128,153]{0,1:T(8,128)}, f32[128,153]{0,1:T(8,128)}), (f32[2,96,1024]{2,1,0:T(8,128)}, f32[128,153]{0,1:T(8,128)}, f32[128,153]{0,1:T(8,128)})) %all-reduce.5.cloned.1.call-update) | async-done | bytes 943120 | tf_op jit(solution)/shard_map/psum | solution.py:114
  (235 shorter events, 315.4 us)
Async XLA Ops:
  7.2 1211.2 %copy-start = (bf16[128,153]{0,1:T(8,128)(2,1)S(1)}, bf16[128,153]{0,1:T(8,128)(2,1)}, u32[]{:S(2)}) copy-start(bf16[128,153]{0,1:T(8,128)(2,1)} %param.30) | copy-start | bytes 117508
  7.2 1209.9 %reduce-scatter.2.cloned.1.call-start = ((), (), s32[]{:S(2)}) async-start(), calls=%async_computation.1 | async-start | bytes 16908288 | tf_op jit(solution)/shard_map/reduce_scatter | solution.py:56
  14.6 439.1 %copy-start.4 = (bf16[96,1024]{1,0:T(8,128)(2,1)S(1)}, bf16[96,1024]{1,0:T(8,128)(2,1)}, u32[]{:S(2)}) copy-start(bf16[96,1024]{1,0:T(8,128)(2,1)} %param.27) | copy-start | bytes 589828
  450.6 1.3 copy-start.1
  479.8 5.8 copy-start.5
  492.9 20.9 %copy-start.2 = (f32[128,96,128]{2,1,0:T(8,128)S(1)}, f32[128,96,128]{2,1,0:T(8,128)}, u32[]{:S(2)}) copy-start(f32[128,96,128]{2,1,0:T(8,128)} %gather_fusion.3) | copy-start | bytes 18874372
  548.1 0.8 copy-start.7
  548.1 668.9 %copy-start.9 = (f32[128]{0:T(128)S(1)}, f32[128]{0:T(128)}, u32[]{:S(2)}) copy-start(f32[128]{0:T(128)} %param.28) | copy-start | bytes 1540
  548.1 670.1 %copy-start.6 = (bf16[128,153]{0,1:T(8,128)(2,1)S(1)}, bf16[128,153]{0,1:T(8,128)(2,1)}, u32[]{:S(2)}) copy-start(bf16[128,153]{0,1:T(8,128)(2,1)} %param.29) | copy-start | bytes 117508
  548.1 694.1 %copy-start.8 = (f32[153]{0:T(256)S(1)}, f32[153]{0:T(256)}, u32[]{:S(2)}) copy-start(f32[153]{0:T(256)} %param.31) | copy-start | bytes 1840
  548.1 694.2 %copy-start.10 = (s32[1,32]{1,0:T(1,128)S(1)}, s32[1,32]{1,0:T(1,128)}, u32[]{:S(2)}) copy-start(s32[1,32]{1,0:T(1,128)} %param.25) | copy-start | bytes 388
  548.2 772.0 %all-gather.3.cloned.1.call-start = ((), (), s32[]{:S(2)}) async-start(), calls=%async_computation.2 | async-start | bytes 16908288 | tf_op jit(solution)/shard_map/all_gather | solution.py:96
  1218.1 121.9 %copy-start.3 = (bf16[256,128]{1,0:T(8,128)(2,1)}, bf16[256,128]{1,0:T(8,128)(2,1)S(1)}, u32[]{:S(2)}) copy-start(bf16[256,128]{1,0:T(8,128)(2,1)S(1)} %select_convert_fusion) | copy-start | bytes 196612
  1244.8 228.1 %all-reduce.5.cloned.1.call-start = ((), (), s32[]{:S(2)}) async-start(), calls=%async_computation.3 | async-start | bytes 1900544 | tf_op jit(solution)/shard_map/psum | solution.py:114
Sparse Core Ops, SparseCore 0:
  548.3 668.6 reduce-scatter.1
  1244.9 75.2 all-gather.2
  1387.1 85.7 all-reduce.4
where the time goes:
time: 1490 us
  waiting for transfers between devices  785 us (53%)
  local copies, waits for them, and re-layouts  395 us (27%)
  matrix products  126 us (8%)
  other arithmetic  97.2 us (7%)
  blocking collectives  64.7 us (4%)
  between operations  16.5 us (1%)
    reduce_scatter x1, waiting for transfers between devices, body(): lax.psum_scatter(jnp.einsum('fct,cfh->cth', self_pick, jnp.take(self_bloc...  668 us
    gather x27, local copies, waits for them, and re-layouts, local_cols(): cols = jnp.take(node_features, jnp.clip(local, 0, node_rows - 1), axis=1)  362 us
    all_gather x1, waiting for transfers between devices, body(): piece = lax.all_gather(grad_pre[None], ('group', 'mp'), axis=0, tiled=True)  73.3 us
    psum x1, waiting for transfers between devices, body(): lax.psum((local_terms[0], local_terms[1], local_terms[2], local_terms[3],...  43.4 us
    psum x1, blocking collectives, body(): lax.psum((local_terms[0], local_terms[1], local_terms[2], local_terms[3],...  41.1 us
    dot_general x2, matrix products, body(): jnp.einsum('fct,cth,cm->fmh', neigh_pick, piece, select, precision=high)  39.2 us
    add x25, other arithmetic, add_slot(): return (running + local_cols(node_ids), None)  35.7 us
    dot_general x1, matrix products, body(): jnp.einsum('fct,cfh->cth', self_pick, jnp.take(self_blocks, column, axis=...  34.4 us
  transfers between devices with their start and end apart: 3, of which 3 were waited for; matrix products, arithmetic and copies ran while one was open for 0% of the time, Pallas kernels for 0%

commit v1 on v0

v1 whole, which is shorter than its diff:
```python
import functools
import jax
import jax.numpy as jnp
from jax import lax
from jax.experimental import pallas as pl
from jax.experimental.pallas import tpu as pltpu
from jax.sharding import PartitionSpec as P

UNROLL = 16

def gather_kernel(feat_ref, ids_ref, out_ref, table, acc, codes, first, counts, first_s, counts_s, extra_s, sems):
    nodes = feat_ref.shape[1]
    width = feat_ref.shape[0]
    chunks = ids_ref.shape[0]
    slots = acc.shape[0] - 8
    half = slots // 2
    per_half = half // 1024
    lane = lax.broadcasted_iota(jnp.int32, (8, 8, 128), 2)
    sub = lax.broadcasted_iota(jnp.int32, (8, 8, 128), 1)
    outer = lax.broadcasted_iota(jnp.int32, (8, 8, 128), 0)
    row_i = lax.broadcasted_iota(jnp.int32, (128, 128), 0)
    col_i = lax.broadcasted_iota(jnp.int32, (128, 128), 1)
    before = jnp.where(row_i < col_i, 1.0, 0.0).astype(jnp.bfloat16)
    ones = jnp.ones((128, 128), jnp.bfloat16)
    shift = (nodes - 1).bit_length()
    flag = 1 << (shift + 10)

    def compact(q, carry):
        local = ids_ref[pl.ds(q * 8, 8)]
        inside = (local >= 0) & (local < nodes)
        out_f = jnp.where(inside, 0.0, 1.0)
        out_b = out_f.reshape(64, 128).astype(jnp.bfloat16)
        pref = jnp.dot(out_b, before, preferred_element_type=jnp.float32).reshape(8, 8, 128)
        total = jnp.dot(out_b, ones, preferred_element_type=jnp.float32).reshape(8, 8, 128)
        scan = jnp.where(sub >= 1, pltpu.roll(total, 1, 1), 0.0)
        for step in (1, 2, 4):
            scan = scan + jnp.where(sub >= step, pltpu.roll(scan, step, 1), 0.0)
        moved = (pref + scan).astype(jnp.int32)
        counts[pl.ds(q * 8, 8), :] = 1024 - jnp.sum(total, axis=1).astype(jnp.int32)
        x = jnp.where(inside, flag | (moved << shift) | local, 0)
        for j in range(10):
            d = 1 << j
            if j < 7:
                y = pltpu.roll(x, 128 - d, 2)
                y = jnp.where(lane < 128 - d, y, pltpu.roll(y, 7, 1))
            else:
                y = pltpu.roll(x, 8 - d // 128, 1)
            bit = 1 << (shift + j)
            x = jnp.where((y & bit) != 0, y, jnp.where((x & bit) != 0, 0, x))
        chunk = q * 8 + outer
        slot = sub * 128 + lane + ((x >> shift) & 1023) + (chunk % per_half) * 1024
        slot = slot + jnp.where(chunk >= chunks - per_half, half, 0)
        code = jnp.where(x != 0, (slot << 15) | (x & (nodes - 1)), (slots << 15) | nodes)
        codes[pl.ds(q * 8, 8)] = code
        first[pl.ds(q * 8, 8), :] = codes[pl.ds(q * 8, 8), 0, :]
        return carry

    lax.fori_loop(0, chunks // 8, compact, 0)
    copy_first = pltpu.make_async_copy(first, first_s, sems.at[0])
    copy_counts = pltpu.make_async_copy(counts, counts_s, sems.at[1])
    copy_first.start()
    copy_counts.start()

    def turn(i, carry):
        at = pl.multiple_of(i * 128, 128)
        block = feat_ref[:, pl.ds(at, 128)].astype(jnp.float32)
        block = jnp.concatenate([block, jnp.zeros((128 - width, 128), jnp.float32)], axis=0)
        table[pl.ds(at, 128), :] = block.T
        return carry

    lax.fori_loop(0, nodes // 128, turn, 0, unroll=4)
    table[pl.ds(nodes, 8), :] = jnp.zeros((8, 128), jnp.float32)

    def clear(i, carry):
        acc[pl.ds(pl.multiple_of(i * 64, 64), 64), :] = jnp.zeros((64, 128), jnp.float32)
        return carry

    lax.fori_loop(0, slots // 64, clear, 0)
    acc[pl.ds(slots, 8), :] = jnp.zeros((8, 128), jnp.float32)
    copy_first.wait()
    copy_counts.wait()

    def add_rows(read, n):
        def group(i, carry):
            code = [read(i * UNROLL + u) for u in range(UNROLL)]
            at = [c >> 15 for c in code]
            rows = [table[pl.ds(c & 32767, 1), :] for c in code]
            olds = [acc[pl.ds(a, 1), :] for a in at]
            for a, old, row in zip(at, olds, rows):
                acc[pl.ds(a, 1), :] = old + row
            return carry

        lax.fori_loop(0, (n + UNROLL - 1) // UNROLL, group, 0)

    def chunk_rows(j, carry):
        n = counts_s[j, 0]
        add_rows(lambda i: first_s[j, i], jnp.minimum(n, 128))

        @pl.when(n > 128)
        def _():
            copy = pltpu.make_async_copy(codes.at[j], extra_s, sems.at[2])
            copy.start()
            copy.wait()

            def rest(r, inner):
                add_rows(lambda i: extra_s[r, i], jnp.minimum(n - r * 128, 128))
                return inner

            lax.fori_loop(1, (n + 127) // 128, rest, 0)

        return carry

    lax.fori_loop(0, chunks, chunk_rows, 0)

    lanes = lax.broadcasted_iota(jnp.int32, (64, 128), 1)

    def pack(i, carry):
        for s in range(2):
            base = (1 - s) * half + i * 256
            a, b, c, d = [acc[pl.ds(pl.multiple_of(base + n * 64, 64), 64), :] for n in range(4)]
            b, c, d = pltpu.roll(b, 96, 1), pltpu.roll(c, 64, 1), pltpu.roll(d, 32, 1)
            out_ref[i, pl.ds(s * 192, 64), :] = jnp.where(lanes < 96, a, b)
            out_ref[i, pl.ds(s * 192 + 64, 64), :] = jnp.where(lanes < 64, b, c)
            out_ref[i, pl.ds(s * 192 + 128, 64), :] = jnp.where(lanes < 32, c, d)
        return carry

    lax.fori_loop(0, half // 256, pack, 0)


def gather_rows(features, local_ids, batches):
    nodes = features.shape[1]
    chunks = local_ids.shape[0]
    return pl.pallas_call(
        gather_kernel,
        out_shape=jax.ShapeDtypeStruct((batches, 384, 128), jnp.float32),
        in_specs=[pl.BlockSpec(memory_space=pltpu.VMEM)] * 2,
        out_specs=pl.BlockSpec(memory_space=pltpu.VMEM),
        scratch_shapes=[
            pltpu.VMEM((nodes + 8, 128), jnp.float32),
            pltpu.VMEM((batches * 512 + 8, 128), jnp.float32),
            pltpu.VMEM((chunks, 8, 128), jnp.int32),
            pltpu.VMEM((chunks, 128), jnp.int32),
            pltpu.VMEM((chunks, 128), jnp.int32),
            pltpu.SMEM((chunks, 128), jnp.int32),
            pltpu.SMEM((chunks, 128), jnp.int32),
            pltpu.SMEM((8, 128), jnp.int32),
            pltpu.SemaphoreType.DMA((3,)),
        ],
        compiler_params=pltpu.CompilerParams(vmem_limit_bytes=48 * 1024 * 1024),
        name="gather_rows",
    )(features, local_ids)


def local_ids_of(target_nodes, first_hop, offset):
    ids = jnp.concatenate([jnp.moveaxis(first_hop, 1, 0), target_nodes[None]], axis=0) - offset
    return ids.reshape(-1, 8, 128)


MESH = pl.DeviceIdType.MESH
HIGH = lax.Precision.HIGHEST


def run_all(*routes):
    active = list(routes)
    while active:
        for route in list(active):
            try:
                next(route)
            except StopIteration:
                active.remove(route)


def ring_sum(blk, inb, ssem, rsem, base, i, right, left):
    after, before, across = lax.rem(i + 1, 4), lax.rem(i + 3, 4), lax.rem(i + 2, 4)

    def copy(src, k, device):
        return pltpu.make_async_remote_copy(
            src_ref=src,
            dst_ref=inb(k),
            send_sem=ssem.at[base + k],
            recv_sem=rsem.at[base + k],
            device_id=device,
            device_id_type=MESH,
        )

    c0 = copy(blk(across, 0), 0, right)
    c1 = copy(blk(across, 1), 1, left)
    c2 = copy(blk(after, 1), 2, right)
    c3 = copy(blk(before, 0), 3, left)
    c4 = copy(blk(after, 0), 4, right)
    c5 = copy(blk(before, 1), 5, left)
    for c in (c0, c1, c2, c3):
        c.start()
    yield
    c0.wait_recv()
    blk(after, 0)[...] = blk(after, 0)[...] + inb(0)[...]
    c4.start()
    c1.wait_recv()
    blk(before, 1)[...] = blk(before, 1)[...] + inb(1)[...]
    c5.start()
    yield
    c3.wait_recv()
    c2.wait_recv()
    blk(i, 0)[...] = blk(i, 0)[...] + inb(3)[...]
    blk(i, 1)[...] = blk(i, 1)[...] + inb(2)[...]
    yield
    c4.wait_recv()
    blk(i, 0)[...] = blk(i, 0)[...] + inb(4)[...]
    c5.wait_recv()
    blk(i, 1)[...] = blk(i, 1)[...] + inb(5)[...]
    for c in (c0, c1, c2, c3, c4, c5):
        c.wait_send()


def ring_gather(blk, part, ssem, rsem, base, i, right, left, landed=None):
    after, before, across = lax.rem(i + 1, 4), lax.rem(i + 3, 4), lax.rem(i + 2, 4)

    def copy(ref, k, device):
        return pltpu.make_async_remote_copy(
            src_ref=ref,
            dst_ref=ref,
            send_sem=ssem.at[base + k],
            recv_sem=rsem.at[base + k],
            device_id=device,
            device_id_type=MESH,
        )

    c0 = copy(blk(i), 0, right)
    c1 = copy(blk(i), 1, left)
    c0.start()
    c1.start()
    yield
    c0.wait_recv()
    c2 = copy(part(before, 0), 2, right)
    c2.start()
    c1.wait_recv()
    c3 = copy(part(after, 1), 3, left)
    c3.start()
    if landed is not None:
        landed(0, before)
        landed(1, after)
    yield
    c2.wait_recv()
    c3.wait_recv()
    if landed is not None:
        landed(2, across)
    for c in (c0, c1, c2, c3):
        c.wait_send()


def grid_sum(buf, rows, in_wide, in_thin, ssem, rsem, base, x, y, xs, ys):
    half = rows // 2
    quarter = half // 2

    def route(h):
        lo = h * half

        def wide(d, p):
            at = pl.ds(lo + p * quarter, quarter)
            return buf.at[d, :, at] if h == 0 else buf.at[:, d, at]

        def thin(d, p):
            at = pl.ds(lo + p * quarter, quarter)
            return buf.at[x, d, at] if h == 0 else buf.at[d, y, at]

        first, second = ((x,) + xs, (y,) + ys) if h == 0 else ((y,) + ys, (x,) + xs)
        yield from ring_sum(wide, lambda k: in_wide.at[h, k], ssem, rsem, base + h * 12, *first)
        yield from ring_sum(thin, lambda k: in_thin.at[h, k], ssem, rsem, base + h * 12 + 6, *second)

    return route(0), route(1)


def grid_gather(buf, rows, ssem, rsem, base, x, y, xs, ys):
    half = rows // 2
    quarter = half // 2

    def route(h):
        lo = h * half

        def thin_at(d, at):
            return buf.at[x, d, at] if h == 0 else buf.at[d, y, at]

        def wide_at(d, at):
            return buf.at[d, :, at] if h == 0 else buf.at[:, d, at]

        first, second = ((y,) + ys, (x,) + xs) if h == 0 else ((x,) + xs, (y,) + ys)
        for n, (at_of, ring) in enumerate(((thin_at, first), (wide_at, second))):
            yield from ring_gather(
                lambda d, at_of=at_of: at_of(d, pl.ds(lo, half)),
                lambda d, p, at_of=at_of: at_of(d, pl.ds(lo + p * quarter, quarter)),
                ssem,
                rsem,
                base + h * 8 + n * 4,
                *ring,
            )

    return route(0), route(1)


def unpack(ref, x, y, row, lane64):
    p = [ref[x, y, pl.ds(row + 64 * n, 64), :] for n in range(3)]
    b = jnp.where(lane64 < 32, pltpu.roll(p[0], 32, 1), pltpu.roll(p[1], 32, 1))
    c = jnp.where(lane64 < 64, pltpu.roll(p[1], 64, 1), pltpu.roll(p[2], 64, 1))
    d = pltpu.roll(p[2], 96, 1)
    out = [jnp.where(lane64 < 96, v, 0.0) for v in (p[0], b, c, d)]
    return jnp.concatenate(out, axis=0)


def split(v):
    hi = v.astype(jnp.bfloat16)
    return hi, (v - hi.astype(jnp.float32)).astype(jnp.bfloat16)


def dot(a, b):
    return jnp.dot(a, b, preferred_element_type=jnp.float32)


def high_dot(a, b, dims=((1,), (0,))):
    return lax.dot_general(a, b, (dims, ((), ())), precision=HIGH, preferred_element_type=jnp.float32)


def exchange_kernel(
    fan_one,
    fan_two,
    parts_ref,
    ws_ref,
    wn_ref,
    hb_ref,
    cs_ref,
    cn_ref,
    cb_ref,
    live_ref,
    links_ref,
    labels_ref,
    hidden_ref,
    grads_ref,
    extras_ref,
    parts,
    in_wide,
    in_thin,
    weights,
    pre_parts,
    in_core,
    in_z,
    cs_pad,
    cn_pad,
    logit_own,
    logit_core,
    logit_z,
    piece,
    terms,
    in_wide_t,
    in_thin_t,
    extras,
    in_wide_e,
    in_thin_e,
    local_sem,
    ssem,
    rsem,
):
    group = lax.axis_index("group")
    m = lax.axis_index("mp")
    x, y = lax.div(group, 4), lax.rem(group, 4)
    z, core = lax.div(m, 2), lax.rem(m, 2)

    def device(nx, ny, nz, nc):
        return (nx * 4 + ny, nz * 2 + nc)

    def up(i, n):
        return lax.rem(i + n, 4)

    xs = (device(up(x, 1), y, z, core), device(up(x, 3), y, z, core))
    ys = (device(x, up(y, 1), z, core), device(x, up(y, 3), z, core))
    zs = (device(x, y, up(z, 1), core), device(x, y, up(z, 3), core))
    opposite = device(x, y, up(z, 2), core)
    sibling = device(x, y, z, 1 - core)

    load = pltpu.make_async_copy(parts_ref, parts, local_sem)
    load.start()
    barrier = pltpu.get_barrier_semaphore()
    for near in xs + ys + zs + (opposite, sibling):
        pl.semaphore_signal(barrier, inc=1, device_id=near, device_id_type=MESH)
    pl.semaphore_wait(barrier, 8)
    load.wait()

    used = 0
    rows_sum = grid_sum(parts, 384, in_wide, in_thin, ssem, rsem, used, x, y, xs, ys)
    used += 24
    for route in rows_sum:
        next(route)

    width = ws_ref.shape[0]
    hidden_all = ws_ref.shape[1]
    targets = hidden_ref.shape[0]
    seeds = labels_ref.shape[0]
    classes = cs_ref.shape[1]
    weights[...] = jnp.zeros_like(weights)
    weights[0:width, :] = ws_ref[...]
    weights[128 : 128 + width, :] = wn_ref[...]
    weights[256 : 256 + width, :] = wn_ref[...]
    cs_pad[...] = jnp.zeros_like(cs_pad)
    cn_pad[...] = jnp.zeros_like(cn_pad)
    cs_pad[:, 0:classes] = cs_ref[...].astype(jnp.float32)
    cn_pad[:, 0:classes] = cn_ref[...].astype(jnp.float32)
    target_rows = lax.broadcasted_iota(jnp.int32, (targets, 128), 0)
    links_t = jnp.zeros((targets, 128), jnp.float32)
    for k in range(fan_two):
        links_t = links_t + jnp.where(target_rows == links_ref[k : k + 1, :], 1.0, 0.0)
    links_f = links_t.T[0:seeds]
    run_all(*rows_sum)

    lane64 = lax.broadcasted_iota(jnp.int32, (64, 128), 1)
    self_rows = unpack(parts, x, y, 0, lane64)
    neigh_rows = unpack(parts, x, y, 192, lane64) / fan_one
    neigh_hi, neigh_lo = split(neigh_rows)
    left_side = jnp.concatenate([self_rows.astype(jnp.bfloat16), neigh_hi, neigh_lo], axis=1)
    hid = hidden_ref.shape[1]
    for zz in range(4):
        for cc in range(2):
            at = (zz * 2 + cc) * hid
            pre_parts[zz, cc] = dot(left_side, weights[:, at : at + hid])

    def core_copy(src, dst, k):
        return pltpu.make_async_remote_copy(
            src_ref=src,
            dst_ref=dst,
            send_sem=ssem.at[k],
            recv_sem=rsem.at[k],
            device_id=sibling,
            device_id_type=MESH,
        )

    halves = core_copy(pre_parts.at[:, 1 - core], in_core, used)
    used += 1
    halves.start()
    self_t = self_rows.T[0:width]
    neigh_t = neigh_rows.T[0:width]
    neigh_t_hi, neigh_t_lo = split(neigh_t)
    rows_hi = jnp.concatenate([self_t.astype(jnp.bfloat16), neigh_t_hi], axis=0)
    halves.wait()
    for zz in range(4):
        pre_parts[zz, core] = pre_parts[zz, core] + in_core[zz]
    half_rows = targets // 2
    run_all(
        ring_sum(
            lambda d, p: pre_parts.at[d, core, pl.ds(p * half_rows, half_rows)],
            lambda k: in_z.at[k],
            ssem,
            rsem,
            used,
            z,
            *zs,
        )
    )
    used += 6
    pre = pre_parts[z, core] + hb_ref[...]
    alive = (target_rows < live_ref[0]) & (pre > 0.0)
    hidden = jnp.where(alive, pre, 0.0).astype(jnp.bfloat16)
    hidden_ref[...] = hidden
    active = hidden.astype(jnp.float32)
    seed_self = active[0:seeds]
    seed_neigh = dot(links_f.astype(jnp.bfloat16), hidden) / fan_two
    logit_own[...] = high_dot(seed_self, cs_pad[...]) + high_dot(seed_neigh, cn_pad[...])
    to_core = core_copy(logit_own, logit_core, used)
    used += 1
    to_core.start()
    to_core.wait()
    logit_z[z] = logit_own[...] + logit_core[...]
    sends = []
    for k, near in enumerate(zs + (opposite,)):
        sends.append(
            pltpu.make_async_remote_copy(
                src_ref=logit_z.at[z],
                dst_ref=logit_z.at[z],
                send_sem=ssem.at[used + k],
                recv_sem=rsem.at[used + k],
                device_id=near,
                device_id_type=MESH,
            )
        )
    used += 3
    for c in sends:
        c.start()
    extras[...] = jnp.zeros_like(extras)
    for c in sends:
        c.wait()
    logits = (logit_z[0] + logit_z[1]) + (logit_z[2] + logit_z[3]) + cb_ref[...]
    lanes = lax.broadcasted_iota(jnp.int32, logits.shape, 1)
    logits = jnp.where(lanes < classes, logits, -1e30)
    top = jnp.max(logits, axis=1, keepdims=True)
    log_total = jnp.log(jnp.sum(jnp.exp(logits - top), axis=1, keepdims=True)) + top
    onehot = jnp.where(lanes == labels_ref[...], 1.0, 0.0)
    losses = log_total - jnp.sum(onehot * logits, axis=1, keepdims=True)
    dlogit = jnp.exp(logits - log_total) - onehot
    back_self = high_dot(dlogit, cs_pad[...], ((1,), (1,)))
    back_neigh = high_dot(dlogit, cn_pad[...], ((1,), (1,))) / fan_two
    back_neigh = jnp.concatenate([back_neigh, jnp.zeros((128 - seeds, hid), jnp.float32)], axis=0)
    grad_act = high_dot(links_t, back_neigh)
    grad_act = grad_act + jnp.concatenate(
        [back_self, jnp.zeros((targets - seeds, hid), jnp.float32)], axis=0
    )
    grad_pre = jnp.where(alive, grad_act, 0.0)
    piece[z, core] = grad_pre

    to_sibling = [core_copy(piece.at[z, core], piece.at[z, core], used)]
    to_sibling[0].start()

    def landed(n, d):
        c = core_copy(piece.at[d, core], piece.at[d, core], base_core + 1 + n)
        c.start()
        to_sibling.append(c)

    base_core = used
    used += 4
    spread = ring_gather(
        lambda d: piece.at[d, core],
        lambda d, p: piece.at[d, core, pl.ds(p * half_rows, half_rows)],
        ssem,
        rsem,
        used,
        z,
        *zs,
        landed=landed,
    )
    used += 4
    next(spread)

    dlogit_t = dlogit.T[0:160]
    class_grads = jnp.concatenate(
        [high_dot(dlogit_t, seed_self), high_dot(dlogit_t, seed_neigh)], axis=0
    )
    for n in range(10):
        extras[n // 4, n % 4] = class_grads[n * 32 : n * 32 + 32]
    row_sum = jnp.sum(dlogit, axis=0, keepdims=True)
    extras[2, 2, 0:1] = jnp.sum(grad_pre, axis=0, keepdims=True)
    extras[2, 2, 1:2] = row_sum[:, 0:128]
    extras[2, 2, 2:3] = row_sum[:, 128:256]
    extras[2, 2, 3:4] = jnp.broadcast_to(jnp.sum(losses, axis=0, keepdims=True), (1, 128))
    extra_sum = grid_sum(extras, 32, in_wide_e, in_thin_e, ssem, rsem, used, x, y, xs, ys)
    used += 24
    run_all(spread, *extra_sum)
    extras_ref[x, y] = extras[x, y]
    extra_gather = grid_gather(extras_ref, 32, ssem, rsem, used, x, y, xs, ys)
    used += 16
    for route in extra_gather:
        next(route)
    for c in to_sibling:
        c.wait()
    for zz in range(4):
        for cc in range(2):
            g_hi, g_lo = split(piece[zz, cc])
            term = dot(rows_hi, g_hi) + dot(rows_hi, g_lo)
            terms[zz, 2 * cc] = term[0:width]
            terms[zz, 2 * cc + 1] = term[width : 2 * width] + dot(neigh_t_lo, g_hi)
    term_sum = grid_sum(terms, 96, in_wide_t, in_thin_t, ssem, rsem, used, x, y, xs, ys)
    used += 24
    run_all(*extra_gather, *term_sum)
    grads_ref[x, y] = terms[x, y]
    run_all(*grid_gather(grads_ref, 96, ssem, rsem, used, x, y, xs, ys))
    used += 16
    assert used <= SEMS


SEMS = 160


def body(
    node_features,
    target_nodes,
    first_hop,
    live_counts,
    seed_links,
    seed_labels,
    self_weight,
    neigh_weight,
    hidden_bias,
    class_self,
    class_neigh,
    class_bias,
):
    node_rows = node_features.shape[1]
    batches, targets = target_nodes.shape
    fan_one = first_hop.shape[1]
    seeds, fan_two = seed_links.shape[1:]
    hid = hidden_bias.shape[0]
    width, hidden_all = self_weight.shape
    classes = class_bias.shape[0]
    group = lax.axis_index("group")
    ids = local_ids_of(target_nodes, first_hop, group * node_rows)
    parts = gather_rows(node_features, ids, batches).reshape(4, 4, 384, 128)
    links = jnp.pad(seed_links[0].T, ((0, 1), (0, 128 - seeds)), constant_values=-1)
    labels = seed_labels[0][:, None]
    bias = jnp.pad(class_bias[None], ((0, 0), (0, 256 - classes)))
    f32, vmem = jnp.float32, pl.BlockSpec(memory_space=pltpu.VMEM)
    shapes = [
        ((4, 4, 384, 128), f32),
        ((2, 6, 4, 96, 128), f32),
        ((2, 6, 96, 128), f32),
        ((384, hidden_all), jnp.bfloat16),
        ((4, 2, targets, hid), f32),
        ((4, targets, hid), f32),
        ((6, targets // 2, hid), f32),
        ((hid, 256), f32),
        ((hid, 256), f32),
        ((seeds, 256), f32),
        ((seeds, 256), f32),
        ((4, seeds, 256), f32),
        ((4, 2, targets, hid), f32),
        ((4, 4, 96, 128), f32),
        ((2, 6, 4, 24, 128), f32),
        ((2, 6, 24, 128), f32),
        ((4, 4, 32, 128), f32),
        ((2, 6, 4, 8, 128), f32),
        ((2, 6, 8, 128), f32),
    ]
    hidden_layer, grads, extras = pl.pallas_call(
        functools.partial(exchange_kernel, fan_one, fan_two),
        out_shape=(
            jax.ShapeDtypeStruct((targets, hid), jnp.bfloat16),
            jax.ShapeDtypeStruct((4, 4, 96, 128), f32),
            jax.ShapeDtypeStruct((4, 4, 32, 128), f32),
        ),
        in_specs=[pl.BlockSpec(memory_space=pl.ANY)]
        + [vmem] * 6
        + [pl.BlockSpec(memory_space=pltpu.SMEM)]
        + [vmem] * 2,
        out_specs=(vmem, vmem, vmem),
        scratch_shapes=[pltpu.VMEM(shape, kind) for shape, kind in shapes]
        + [
            pltpu.SemaphoreType.DMA,
            pltpu.SemaphoreType.DMA((SEMS,)),
            pltpu.SemaphoreType.DMA((SEMS,)),
        ],
        compiler_params=pltpu.CompilerParams(
            collective_id=0, has_side_effects=True, vmem_limit_bytes=48 * 1024 * 1024
        ),
        name="exchange",
    )(
        parts,
        self_weight,
        neigh_weight,
        hidden_bias[None],
        class_self,
        class_neigh,
        bias,
        live_counts,
        links,
        labels,
    )
    pair = grads.reshape(8, 2, width, hid)
    rows = extras.reshape(-1, hid)
    both = jnp.moveaxis(pair, 0, 2).reshape(2, width, 8 * hid)
    last = rows[320:324]
    return (
        hidden_layer,
        both[0],
        both[1],
        last[0],
        rows[0:classes].T,
        rows[160 : 160 + classes].T,
        last[1:3].reshape(-1)[0:classes],
        last[3, 0] / (batches * seeds),
    )


def solution(mesh):
    in_specs = (
        P("mp", "group"),
        P(),
        P(),
        P("group"),
        P("group", None, None),
        P("group", None),
        P("mp", None),
        P("mp", None),
        P("mp"),
        P("mp", None),
        P("mp", None),
        P(),
    )
    out_specs = (
        P("group", "mp"),
        P("mp", None),
        P("mp", None),
        P("mp"),
        P("mp", None),
        P("mp", None),
        P(),
        P(),
    )
    return jax.shard_map(body, mesh=mesh, in_specs=in_specs, out_specs=out_specs, check_vma=False)
```

time: 1490 us -> 164 us (0.11)
  waiting for transfers between devices: 785 us -> 0 us
  local copies, waits for them, and re-layouts: 395 us -> 8.36 us
  Pallas kernels: 0 us -> 151 us
  matrix products: 126 us -> 0 us
  other arithmetic: 97.2 us -> 1.05 us
  blocking collectives: 64.7 us -> 0 us
    reduce_scatter x1 -> x0, waiting for transfers between devices: 668 us -> none  [body(): lax.psum_scatter(jnp.einsum('fct,cfh->cth', self_pick, jnp.take(self_bloc...]
    gather x31 -> x0, local copies, waits for them, and re-layouts: 383 us -> none  [the longest x27 362 us: local_cols(): cols = jnp.take(node_features, jnp.clip(local, 0, node_rows - 1), axis=1)]
    pallas_call x0 -> x2, Pallas kernels: none -> 151 us  [the longest x1 103 us: body(): pl.pallas_call(functools.partial(exchange_kernel, fan_one, fan_two), out_...]
    dot_general x14 -> x0, matrix products: 126 us -> none  [the longest x2 39.2 us: body(): jnp.einsum('fct,cth,cm->fmh', neigh_pick, piece, select, precision=high)]
    all_gather x1 -> x0, waiting for transfers between devices: 73.3 us -> none  [body(): piece = lax.all_gather(grad_pre[None], ('group', 'mp'), axis=0, tiled=True)]
    psum x2 -> x0, blocking collectives: 64.7 us -> none  [the longest x1 41.1 us: body(): lax.psum((local_terms[0], local_terms[1], local_terms[2], local_terms[3],...]
    psum x1 -> x0, waiting for transfers between devices: 43.4 us -> none  [body(): lax.psum((local_terms[0], local_terms[1], local_terms[2], local_terms[3],...]
    add x25 -> x0, other arithmetic: 35.7 us -> none  [add_slot(): return (running + local_cols(node_ids), None)]
  transfers between devices with their start and end apart: 3 -> 0, of which waited for: 3 -> 0; matrix products, arithmetic and copies ran while one was open for 0% -> 0% of each run, Pallas kernels for 0% -> 0%
where the time goes in v1:
time: 164 us
  Pallas kernels  151 us (92%)
  local copies, waits for them, and re-layouts  8.36 us (5%)
  between operations  3.18 us (2%)
    pallas_call x1, Pallas kernels, body(): pl.pallas_call(functools.partial(exchange_kernel, fan_one, fan_two), out_...  103 us
    pallas_call x1, Pallas kernels, gather_rows(): pl.pallas_call(gather_kernel, out_shape=jax.ShapeDtypeStruct((batches, 38...  48.2 us

profile of v1, /device:TPU:0, one launch (start us, length us, event | category | flops | bytes accessed | tf_op | source)
XLA Modules:
  0.0 163.9 jit_solution(1703379084948158613)
XLA Ops:
  1.3 0.7 pad.8.cb_ref
  2.0 0.7 copy.31
  2.7 0.7 copy.22.labels_ref
  3.4 0.9 copy.20.cs_ref
  4.3 0.9 copy.21.cn_ref
  5.2 1.1 add_subtract_fusion
  6.3 0.0 copy-start
  6.3 0.0 copy-start.1
  6.3 0.0 copy-start.2
  6.3 48.2 %gather_rows.1 = f32[16,384,128]{2,1,0:T(8,128)S(1)} custom-call(bf16[96,16384]{1,0:T(8,128)(2,1)} %feat_ref.1, s32[104,8,128]{2,1,0:T(8,128)S(1)} %sub.12.ids_ref), custom_call_target="tpu_custom_call" | custom-call | tf_op jit(solution)/shard_map/gather_rows/pallas_call | solution.py:133
  54.5 0.0 copy-done
  54.5 0.0 copy-done.1
  54.5 0.0 copy-done.2
  54.5 103.1 %exchange.1 = (bf16[256,128]{1,0:T(8,128)(2,1)S(1)}, f32[4,4,96,128]{3,2,1,0:T(8,128)S(1)}, f32[4,4,32,128]{3,2,1,0:T(8,128)S(1)}) custom-call(f32[4,4,384,128]{3,2,1,0:T(8,128)S(1)} %bitcast.33, bf16[96,1024]{1,0:T(8,128)(2,1)S(1)} %copy-done, bf16[96,1024]{1,0:T(8,128)(2,1)S(1)} %copy-done.1, f32[1,128]{1,0:T(1,128)S(1)} %bitcast.39, ...), custom_call_target="tpu_custom_call" | custom-call | tf_op jit(solution)/shard_map/exchange/pallas_call | solution.py:616
  157.7 0.5 slice.44
  158.9 0.1 fusion
  158.9 0.2 copy.24
  159.2 0.5 slice_bitcast_fusion.3
  159.7 0.6 slice_bitcast_fusion.2
  160.2 0.7 slice_bitcast_fusion
  160.9 0.2 copy.23
  161.1 1.0 copy_bitcast_fusion
  162.2 0.6 copy.34
  (2 shorter events, 0.0 us)
Async XLA Ops:
  6.3 48.2 %copy-start = (bf16[96,1024]{1,0:T(8,128)(2,1)S(1)}, bf16[96,1024]{1,0:T(8,128)(2,1)}, u32[]{:S(2)}) copy-start(bf16[96,1024]{1,0:T(8,128)(2,1)} %ws_ref.1) | copy-start | bytes 589828
  6.3 48.2 %copy-start.1 = (bf16[96,1024]{1,0:T(8,128)(2,1)S(1)}, bf16[96,1024]{1,0:T(8,128)(2,1)}, u32[]{:S(2)}) copy-start(bf16[96,1024]{1,0:T(8,128)(2,1)} %wn_ref.1) | copy-start | bytes 589828
  6.3 48.2 %copy-start.2 = (f32[128]{0:T(128)S(1)}, f32[128]{0:T(128)}, u32[]{:S(2)}) copy-start(f32[128]{0:T(128)} %param.20) | copy-start | bytes 1540

commit v2 on v1

v2 whole, which is shorter than its diff:
```python
import functools
import jax
import jax.numpy as jnp
from jax import lax
from jax.experimental import pallas as pl
from jax.experimental.pallas import tpu as pltpu
from jax.sharding import PartitionSpec as P

UNROLL = 16
TOP = 3
BLOCK = 4
TURNS = 18


def gather_kernel(offset_ref, feat_ref, targets_ref, hops_ref, out_ref, table, acc, ids, codes, counts, first_s, counts_s, extra_s, sems):
    width, nodes = feat_ref.shape
    lists, rows = ids.shape[:2]
    fan, batches, targets = hops_ref.shape
    used = fan + 1
    half = rows * 128
    slots = 2 * half
    cols = targets // 128
    for n in range(cols):
        at, wide = pl.ds(n * batches, batches), slice(n * 128, n * 128 + 128)
        ids[0:fan, at] = hops_ref[:, :, wide] - offset_ref[0]
        ids[fan, at] = targets_ref[:, wide] - offset_ref[0]
    ids[used:lists] = jnp.full((lists - used, rows, 128), -1, jnp.int32)
    lane = lax.broadcasted_iota(jnp.int32, (BLOCK, rows, 128), 2)
    sub = lax.broadcasted_iota(jnp.int32, (BLOCK, rows, 128), 1)
    outer = lax.broadcasted_iota(jnp.int32, (BLOCK, rows, 128), 0)
    row_i = lax.broadcasted_iota(jnp.int32, (128, 128), 0)
    col_i = lax.broadcasted_iota(jnp.int32, (128, 128), 1)
    before = jnp.where(row_i < col_i, 1.0, 0.0).astype(jnp.bfloat16)
    ones = jnp.ones((128, 128), jnp.bfloat16)
    row_r = lax.broadcasted_iota(jnp.int32, (BLOCK * rows, BLOCK * rows), 0)
    col_r = lax.broadcasted_iota(jnp.int32, (BLOCK * rows, BLOCK * rows), 1)
    same = (row_r // rows) == (col_r // rows)
    above = jnp.where(same & (col_r < row_r), 1.0, 0.0).astype(jnp.bfloat16)
    shift = (nodes - 1).bit_length()
    steps = (half - 1).bit_length()
    flag = 1 << (shift + steps)

    def turn(i):
        at = pl.multiple_of(i * 128, 128)
        part = feat_ref[:, pl.ds(at, 128)].astype(jnp.float32)
        part = jnp.concatenate([part, jnp.zeros((128 - width, 128), jnp.float32)], axis=0)
        table[pl.ds(at, 128), :] = part.T

    def compact(q, carry):
        local = ids[pl.ds(q * BLOCK, BLOCK)]
        inside = (local >= 0) & (local < nodes)
        out_b = jnp.where(inside, 0.0, 1.0).reshape(BLOCK * rows, 128).astype(jnp.bfloat16)
        pref = jnp.dot(out_b, before, preferred_element_type=jnp.float32)
        total = jnp.dot(out_b, ones, preferred_element_type=jnp.float32)
        scan = jnp.dot(above, total.astype(jnp.bfloat16), preferred_element_type=jnp.float32)
        moved = (pref + scan).reshape(BLOCK, rows, 128).astype(jnp.int32)
        total = total.reshape(BLOCK, rows, 128)
        for b in range(BLOCK):
            missing = jnp.sum(total[b], axis=0, keepdims=True)
            counts[pl.ds(q * BLOCK + b, 1), :] = (half - missing).astype(jnp.int32)
        x = jnp.where(inside, flag | (moved << shift) | local, 0)
        for j in range(steps):
            d = 1 << j
            if j < 7:
                y = pltpu.roll(x, 128 - d, 2)
                y = jnp.where(lane < 128 - d, y, pltpu.roll(y, rows - 1, 1))
            else:
                y = pltpu.roll(x, rows - d // 128, 1)
            bit = 1 << (shift + j)
            x = jnp.where((y & bit) != 0, y, jnp.where((x & bit) != 0, 0, x))
        place = sub * 128 + lane + ((x >> shift) & (half - 1))
        row = place >> 7
        slot = (row % batches) * targets + (row // batches) * 128 + (place & 127)
        slot = slot + jnp.where(q * BLOCK + outer == fan, half, 0)
        code = jnp.where(x != 0, (slot << 15) | (x & (nodes - 1)), (slots << 15) | nodes)
        codes[pl.ds(q * BLOCK, BLOCK)] = code
        for n in range(TURNS):
            turn(q * TURNS + n)
        return carry

    lax.fori_loop(0, lists // BLOCK, compact, 0)
    copy_counts = pltpu.make_async_copy(counts, counts_s, sems.at[0])
    copy_counts.start()
    copies = []
    for j in range(used):
        for r in range(TOP):
            n = j * TOP + r
            copy = pltpu.make_async_copy(codes.at[j, r], first_s.at[pl.ds(n * 128, 128)], sems.at[n + 2])
            copy.start()
            copies.append(copy)

    def turn_rest(i, carry):
        turn(i)
        return carry

    lax.fori_loop(lists // BLOCK * TURNS, nodes // 128, turn_rest, 0)
    table[pl.ds(nodes, 8), :] = jnp.zeros((8, 128), jnp.float32)

    def clear(i, carry):
        acc[pl.ds(pl.multiple_of(i * 128, 128), 128), :] = jnp.zeros((128, 128), jnp.float32)
        return carry

    lax.fori_loop(0, slots // 128, clear, 0)
    acc[pl.ds(slots, 8), :] = jnp.zeros((8, 128), jnp.float32)
    copy_counts.wait()
    for copy in copies:
        copy.wait()

    def add_group(ref, base):
        code = [ref[base + u] for u in range(UNROLL)]
        at = [c >> 15 for c in code]
        rows = [table[pl.ds(c & 32767, 1), :] for c in code]
        olds = [acc[pl.ds(a, 1), :] for a in at]
        for a, old, row in zip(at, olds, rows):
            acc[pl.ds(a, 1), :] = old + row

    span = TOP * 128

    def step(state):
        j, k = state
        add_group(first_s, j * span + k)
        k = k + UNROLL
        done = k >= jnp.minimum(counts_s[j, 0], span)
        return jnp.where(done, j + 1, j), jnp.where(done, 0, k)

    lax.while_loop(lambda state: state[0] < used, step, (0, 0))

    def rest(j, carry):
        n = counts_s[j, 0]

        @pl.when(n > span)
        def _():
            def one(r, inner):
                copy = pltpu.make_async_copy(codes.at[j, r], extra_s, sems.at[1])
                copy.start()
                copy.wait()

                def group(i, inner2):
                    add_group(extra_s, i * UNROLL)
                    return inner2

                return lax.fori_loop(0, 128 // UNROLL, group, inner)

            lax.fori_loop(TOP, (n + 127) // 128, one, 0)

        return carry

    lax.fori_loop(0, used, rest, 0)

    lanes = lax.broadcasted_iota(jnp.int32, (64, 128), 1)

    def pack(i, carry):
        for s in range(2):
            base = (1 - s) * half + i * 256
            a, b, c, d = [acc[pl.ds(pl.multiple_of(base + n * 64, 64), 64), :] for n in range(4)]
            b, c, d = pltpu.roll(b, 96, 1), pltpu.roll(c, 64, 1), pltpu.roll(d, 32, 1)
            out_ref[i, pl.ds(s * 192, 64), :] = jnp.where(lanes < 96, a, b)
            out_ref[i, pl.ds(s * 192 + 64, 64), :] = jnp.where(lanes < 64, b, c)
            out_ref[i, pl.ds(s * 192 + 128, 64), :] = jnp.where(lanes < 32, c, d)
        return carry

    lax.fori_loop(0, half // 256, pack, 0)


def gather_rows(features, target_nodes, first_hop, offset):
    nodes = features.shape[1]
    batches, targets = target_nodes.shape
    rows = batches * targets // 128
    lists = 28
    vmem = pl.BlockSpec(memory_space=pltpu.VMEM)
    return pl.pallas_call(
        gather_kernel,
        out_shape=jax.ShapeDtypeStruct((batches, 384, 128), jnp.float32),
        in_specs=[pl.BlockSpec(memory_space=pltpu.SMEM)] + [vmem] * 3,
        out_specs=vmem,
        scratch_shapes=[
            pltpu.VMEM((nodes + 8, 128), jnp.float32),
            pltpu.VMEM((batches * 512 + 8, 128), jnp.float32),
            pltpu.VMEM((lists, rows, 128), jnp.int32),
            pltpu.VMEM((lists, rows, 128), jnp.int32),
            pltpu.VMEM((lists + 4, 128), jnp.int32),
            pltpu.SMEM((lists * TOP * 128,), jnp.int32),
            pltpu.SMEM((lists + 4, 128), jnp.int32),
            pltpu.SMEM((128,), jnp.int32),
            pltpu.SemaphoreType.DMA((lists * TOP + 2,)),
        ],
        compiler_params=pltpu.CompilerParams(vmem_limit_bytes=48 * 1024 * 1024),
        name="gather_rows",
    )(offset, features, target_nodes, jnp.moveaxis(first_hop, 1, 0))


MESH = pl.DeviceIdType.MESH
HIGH = lax.Precision.HIGHEST


def run_all(*routes):
    active = list(routes)
    while active:
        for route in list(active):
            try:
                next(route)
            except StopIteration:
                active.remove(route)


def ring_sum(blk, inb, ssem, rsem, base, i, right, left):
    after, before, across = lax.rem(i + 1, 4), lax.rem(i + 3, 4), lax.rem(i + 2, 4)

    def copy(src, k, device):
        return pltpu.make_async_remote_copy(
            src_ref=src,
            dst_ref=inb(k),
            send_sem=ssem.at[base + k],
            recv_sem=rsem.at[base + k],
            device_id=device,
            device_id_type=MESH,
        )

    c0 = copy(blk(across, 0), 0, right)
    c1 = copy(blk(across, 1), 1, left)
    c2 = copy(blk(after, 1), 2, right)
    c3 = copy(blk(before, 0), 3, left)
    c4 = copy(blk(after, 0), 4, right)
    c5 = copy(blk(before, 1), 5, left)
    for c in (c0, c1, c2, c3):
        c.start()
    yield
    c0.wait_recv()
    blk(after, 0)[...] = blk(after, 0)[...] + inb(0)[...]
    c4.start()
    c1.wait_recv()
    blk(before, 1)[...] = blk(before, 1)[...] + inb(1)[...]
    c5.start()
    yield
    c3.wait_recv()
    c2.wait_recv()
    blk(i, 0)[...] = blk(i, 0)[...] + inb(3)[...]
    blk(i, 1)[...] = blk(i, 1)[...] + inb(2)[...]
    yield
    c4.wait_recv()
    blk(i, 0)[...] = blk(i, 0)[...] + inb(4)[...]
    c5.wait_recv()
    blk(i, 1)[...] = blk(i, 1)[...] + inb(5)[...]
    for c in (c0, c1, c2, c3, c4, c5):
        c.wait_send()


def grid_sum(buf, spans, in_wide, in_thin, ssem, rsem, base, x, y, xs, ys):
    def route(n, h, lo, half):
        def wide(d, p):
            at = pl.ds(lo + p * half, half)
            return buf.at[d, :, at] if h == 0 else buf.at[:, d, at]

        def thin(d, p):
            at = pl.ds(lo + p * half, half)
            return buf.at[x, d, at] if h == 0 else buf.at[d, y, at]

        first, second = ((x,) + xs, (y,) + ys) if h == 0 else ((y,) + ys, (x,) + xs)
        yield from ring_sum(wide, lambda k: in_wide.at[n, k], ssem, rsem, base + n * 12, *first)
        yield from ring_sum(thin, lambda k: in_thin.at[n, k], ssem, rsem, base + n * 12 + 6, *second)

    return [route(n, *span) for n, span in enumerate(spans)]


def grid_gather(buf, spans, ssem, rsem, base, x, y, device):
    def route(n, h, lo, rows):
        at = pl.ds(lo, rows)

        def near(dx, dy):
            return device(dx, dy) if h == 0 else device(dy, dx)

        def place(far, close):
            return buf.at[far, close, at] if h == 0 else buf.at[close, far, at]

        far, close = (x, y) if h == 0 else (y, x)
        started = []

        def send(ref, k, target):
            copy = pltpu.make_async_remote_copy(
                src_ref=ref,
                dst_ref=ref,
                send_sem=ssem.at[base + n * 15 + k],
                recv_sem=rsem.at[base + n * 15 + k],
                device_id=target,
                device_id_type=MESH,
            )
            copy.start()
            started.append(copy)

        for d in (1, 3, 2):
            send(place(far, close), d - 1, near(0, d))
        for d in (1, 3, 2):
            send(place(far, close), 2 + d, near(d, 0))
        firsts = list(started)
        for n2, d in enumerate((1, 3, 2)):
            yield
            firsts[n2].wait_recv()
            source = lax.rem(close + 4 - d, 4)
            for e in (1, 3, 2):
                send(place(far, source), 3 * d + 2 + e, near(e, 0))
        yield
        for copy in started[3:]:
            copy.wait_recv()
        for copy in started:
            copy.wait_send()

    return [route(n, *span) for n, span in enumerate(spans)]


def unpack(ref, x, y, row, lane64):
    p = [ref[x, y, pl.ds(row + 64 * n, 64), :] for n in range(3)]
    b = jnp.where(lane64 < 32, pltpu.roll(p[0], 32, 1), pltpu.roll(p[1], 32, 1))
    c = jnp.where(lane64 < 64, pltpu.roll(p[1], 64, 1), pltpu.roll(p[2], 64, 1))
    d = pltpu.roll(p[2], 96, 1)
    out = [jnp.where(lane64 < 96, v, 0.0) for v in (p[0], b, c, d)]
    return jnp.concatenate(out, axis=0)


def split(v):
    hi = v.astype(jnp.bfloat16)
    return hi, (v - hi.astype(jnp.float32)).astype(jnp.bfloat16)


def dot(a, b):
    return jnp.dot(a, b, preferred_element_type=jnp.float32)


def high_dot(a, b, dims=((1,), (0,))):
    return lax.dot_general(a, b, (dims, ((), ())), precision=HIGH, preferred_element_type=jnp.float32)


def exchange_kernel(
    fan_one,
    fan_two,
    parts_ref,
    ws_ref,
    wn_ref,
    hb_ref,
    cs_ref,
    cn_ref,
    cb_ref,
    live_ref,
    links_ref,
    labels_ref,
    hidden_ref,
    sums_ref,
    parts,
    in_wide,
    in_thin,
    weights,
    pre_parts,
    in_core,
    in_z,
    cs_pad,
    cn_pad,
    cb_pad,
    label_rows,
    link_pad,
    logit_own,
    logit_core,
    logit_z,
    piece,
    terms,
    in_terms,
    extras,
    in_extras,
    local_sem,
    ssem,
    rsem,
):
    group = lax.axis_index("group")
    m = lax.axis_index("mp")
    x, y = lax.div(group, 4), lax.rem(group, 4)
    z, core = lax.div(m, 2), lax.rem(m, 2)
    groups = in_terms.shape[0]

    def up(i, n):
        return lax.rem(i + n, 4)

    def grid_device(dx, dy):
        return (up(x, dx) * 4 + up(y, dy), m)

    def z_device(dz):
        return (group, up(z, dz) * 2 + core)

    xs = (grid_device(1, 0), grid_device(3, 0))
    ys = (grid_device(0, 1), grid_device(0, 3))
    zs = (z_device(1), z_device(3))
    opposite = z_device(2)
    sibling = (group, z * 2 + 1 - core)
    others = [(lax.rem(group + r, groups), m) for r in range(1, groups)]

    load = pltpu.make_async_copy(parts_ref, parts, local_sem)
    load.start()
    barrier = pltpu.get_barrier_semaphore()
    nears = others + list(zs) + [opposite, sibling]
    for near in nears:
        pl.semaphore_signal(barrier, inc=1, device_id=near, device_id_type=MESH)
    pl.semaphore_wait(barrier, len(nears))
    load.wait()

    used = 0
    spans = ((0, 0, 48), (1, 192, 48), (0, 96, 48), (1, 288, 48))
    rows_sum = grid_sum(parts, spans, in_wide, in_thin, ssem, rsem, used, x, y, xs, ys)
    used += 48
    for route in rows_sum:
        next(route)

    width = ws_ref.shape[0]
    targets, hid = hidden_ref.shape
    seeds = labels_ref.shape[1]
    classes = cs_ref.shape[0]
    weights[...] = jnp.zeros_like(weights)
    weights[0:width, :] = ws_ref[...]
    weights[128 : 128 + width, :] = wn_ref[...]
    weights[256 : 256 + width, :] = wn_ref[...]
    cs_pad[...] = jnp.zeros_like(cs_pad)
    cn_pad[...] = jnp.zeros_like(cn_pad)
    cb_pad[...] = jnp.zeros_like(cb_pad)
    cs_pad[0:classes, :] = cs_ref[...].astype(jnp.float32)
    cn_pad[0:classes, :] = cn_ref[...].astype(jnp.float32)
    cb_pad[:, 0:classes] = cb_ref[...]
    extras[...] = jnp.zeros_like(extras)
    for s in range(seeds):
        label_rows[s : s + 1, :] = jnp.full((1, 256), labels_ref[0, s], jnp.int32)
    seed_cols = lax.broadcasted_iota(jnp.int32, (targets, seeds), 0)
    counted = jnp.zeros((targets, seeds), jnp.float32)
    for k in range(fan_two):
        counted = counted + jnp.where(seed_cols == links_ref[k], 1.0, 0.0)
    link_pad[...] = jnp.zeros_like(link_pad)
    link_pad[:, 0:seeds] = counted
    links_t = link_pad[...]
    links_f = links_t.T[0:seeds]
    run_all(*rows_sum)

    lane64 = lax.broadcasted_iota(jnp.int32, (64, 128), 1)
    target_rows = lax.broadcasted_iota(jnp.int32, (targets, 128), 0)
    self_rows = unpack(parts, x, y, 0, lane64)
    neigh_rows = unpack(parts, x, y, 192, lane64) / fan_one
    neigh_hi, neigh_lo = split(neigh_rows)
    left_side = jnp.concatenate([self_rows.astype(jnp.bfloat16), neigh_hi, neigh_lo], axis=1)

    def block_of(zz, cc):
        at = pl.multiple_of((zz * 2 + cc) * hid, hid)
        pre_parts[zz, cc] = dot(left_side, weights[:, pl.ds(at, hid)])

    def core_copy(src, dst, k):
        return pltpu.make_async_remote_copy(
            src_ref=src,
            dst_ref=dst,
            send_sem=ssem.at[k],
            recv_sem=rsem.at[k],
            device_id=sibling,
            device_id_type=MESH,
        )

    half_rows = targets // 2

    def owner_sum(n, base):
        at = pl.ds(n * half_rows, half_rows)
        copy = core_copy(pre_parts.at[:, 1 - core, at], in_core.at[:, at], base)
        copy.start()
        yield
        copy.wait()
        for zz in range(4):
            pre_parts[zz, core, at] = pre_parts[zz, core, at] + in_core[zz, at]
        quarter = half_rows // 2
        yield from ring_sum(
            lambda d, p: pre_parts.at[d, core, pl.ds(n * half_rows + p * quarter, quarter)],
            lambda k: in_z.at[n, k],
            ssem,
            rsem,
            base + 1,
            z,
            *zs,
        )

    for zz in range(4):
        block_of(zz, 1 - core)
    owners = [owner_sum(n, used + 7 * n) for n in range(2)]
    used += 14
    for route in owners:
        next(route)
    for zz in range(4):
        block_of(zz, core)
    self_t = self_rows.T[0:width]
    neigh_t = neigh_rows.T[0:width]
    neigh_t_hi, neigh_t_lo = split(neigh_t)
    rows_hi = jnp.concatenate([self_t.astype(jnp.bfloat16), neigh_t_hi], axis=0)
    run_all(*owners)

    pre = pre_parts[z, core] + hb_ref[...]
    alive = (target_rows < live_ref[0]) & (pre > 0.0)
    hidden = jnp.where(alive, pre, 0.0).astype(jnp.bfloat16)
    hidden_ref[...] = hidden
    active = hidden.astype(jnp.float32)
    seed_self = active[0:seeds]
    seed_neigh = dot(links_f.astype(jnp.bfloat16), hidden) / fan_two
    rows_cols = ((1,), (1,))
    logit_own[...] = high_dot(seed_self, cs_pad[...], rows_cols) + high_dot(seed_neigh, cn_pad[...], rows_cols)
    to_core = core_copy(logit_own, logit_core, used)
    used += 1
    to_core.start()
    to_core.wait()
    logit_z[z] = logit_own[...] + logit_core[...]

    def z_sends(ref, base):
        copies = []
        for k, near in enumerate(zs + (opposite,)):
            copies.append(
                pltpu.make_async_remote_copy(
                    src_ref=ref,
                    dst_ref=ref,
                    send_sem=ssem.at[base + k],
                    recv_sem=rsem.at[base + k],
                    device_id=near,
                    device_id_type=MESH,
                )
            )
            copies[-1].start()
        return copies

    sends = z_sends(logit_z.at[z], used)
    used += 3
    for c in sends:
        c.wait()
    logits = (logit_z[0] + logit_z[1]) + (logit_z[2] + logit_z[3]) + cb_pad[...]
    lanes = lax.broadcasted_iota(jnp.int32, logits.shape, 1)
    logits = jnp.where(lanes < classes, logits, -1e30)
    top = jnp.max(logits, axis=1, keepdims=True)
    log_total = jnp.log(jnp.sum(jnp.exp(logits - top), axis=1, keepdims=True)) + top
    onehot = jnp.where(lanes == label_rows[...], 1.0, 0.0)
    losses = log_total - jnp.sum(onehot * logits, axis=1, keepdims=True)
    dlogit = jnp.exp(logits - log_total) - onehot
    back_self = high_dot(dlogit, cs_pad[...])
    back_neigh = high_dot(dlogit, cn_pad[...]) / fan_two
    back_neigh = jnp.concatenate([back_neigh, jnp.zeros((128 - seeds, hid), jnp.float32)], axis=0)
    grad_act = high_dot(links_t, back_neigh)
    grad_act = grad_act + jnp.concatenate(
        [back_self, jnp.zeros((targets - seeds, hid), jnp.float32)], axis=0
    )
    grad_pre = jnp.where(alive, grad_act, 0.0)
    piece[0, 0] = grad_pre

    def piece_send(slot, target, k):
        copy = pltpu.make_async_remote_copy(
            src_ref=piece.at[0, 0],
            dst_ref=piece.at[slot, 0],
            send_sem=ssem.at[used + k],
            recv_sem=rsem.at[used + k],
            device_id=target,
            device_id_type=MESH,
        )
        copy.start()
        return copy

    spread = [piece_send(1, zs[0], 0), piece_send(3, zs[1], 1), piece_send(2, opposite, 2)]
    used += 3
    core_base = used
    used += 4
    to_sibling = [core_copy(piece.at[0, 0], piece.at[0, 1], core_base)]
    to_sibling[0].start()

    dlogit_t = dlogit.T[0:160]
    class_grads = jnp.concatenate(
        [high_dot(dlogit_t, seed_self), high_dot(dlogit_t, seed_neigh)], axis=0
    )
    per = extras.shape[1]
    for n in range(0, 320, 8):
        extras[n // per, n % per : n % per + 8] = class_grads[n : n + 8]
    row_sum = jnp.sum(dlogit, axis=0, keepdims=True)
    lines = (
        jnp.sum(grad_pre, axis=0, keepdims=True),
        row_sum[:, 0:128],
        row_sum[:, 128:256],
        jnp.broadcast_to(jnp.sum(losses, axis=0, keepdims=True), (1, 128)),
    )
    for n, line in enumerate(lines):
        extras[320 // per, 320 % per + n : 320 % per + n + 1] = line
    extra_sends = []
    for r in range(1, groups):
        copy = pltpu.make_async_remote_copy(
            src_ref=extras.at[lax.rem(group + r, groups)],
            dst_ref=in_extras.at[r],
            send_sem=ssem.at[used + r - 1],
            recv_sem=rsem.at[used + r - 1],
            device_id=others[r - 1],
            device_id_type=MESH,
        )
        copy.start()
        extra_sends.append(copy)
    used += groups - 1

    term_base = used
    used += groups

    def term_copy(k, dest, k_recv):
        return pltpu.make_async_remote_copy(
            src_ref=terms.at[k],
            dst_ref=in_terms.at[group],
            send_sem=ssem.at[term_base + k],
            recv_sem=rsem.at[term_base + k_recv],
            device_id=(dest, m),
            device_id_type=MESH,
        )

    dests = {}

    def block_terms(step, n, across):
        zz = lax.rem(z + 4 - n, 4)
        cc = 1 - core if across else core
        g_hi, g_lo = split(piece[n, across])
        term = dot(rows_hi, g_hi) + dot(rows_hi, g_lo)
        terms[2 * step] = term[0:width]
        terms[2 * step + 1] = term[width : 2 * width] + dot(neigh_t_lo, g_hi)
        for s in range(2):
            k = 2 * step + s
            dests[k] = dest = zz * 4 + cc * 2 + s

            @pl.when(dest != group)
            def _():
                term_copy(k, dest, group).start()

            @pl.when(dest == group)
            def _():
                in_terms[group] = terms[k]

    def forward(n):
        copy = core_copy(piece.at[n, 0], piece.at[n, 1], core_base + n)
        copy.start()
        to_sibling.append(copy)

    block_terms(0, 0, 0)
    to_sibling[0].wait_recv()
    block_terms(1, 0, 1)
    spread[0].wait_recv()
    forward(1)
    block_terms(2, 1, 0)
    spread[1].wait_recv()
    forward(3)
    block_terms(3, 3, 0)
    to_sibling[1].wait_recv()
    block_terms(4, 1, 1)
    to_sibling[2].wait_recv()
    block_terms(5, 3, 1)
    spread[2].wait_recv()
    forward(2)
    block_terms(6, 2, 0)
    to_sibling[3].wait_recv()
    block_terms(7, 2, 1)

    for copy in extra_sends:
        copy.wait_recv()
    total = extras[group]
    for r in range(1, groups):
        total = total + in_extras[r]
    sums_ref[x, y, width : width + per] = total
    for source in range(groups):

        @pl.when(source != group)
        def _():
            pltpu.make_async_remote_copy(
                src_ref=terms.at[0],
                dst_ref=in_terms.at[source],
                send_sem=ssem.at[term_base],
                recv_sem=rsem.at[term_base + source],
                device_id=(source, m),
                device_id_type=MESH,
            ).wait_recv()

    total = in_terms[0]
    for source in range(1, groups):
        total = total + in_terms[source]
    sums_ref[x, y, 0:width] = total
    spans = ((0, 0, 56), (1, 56, 64))
    last = grid_gather(sums_ref, spans, ssem, rsem, used, x, y, grid_device)
    used += 30
    for route in last:
        next(route)
    for copy in spread + to_sibling + extra_sends:
        copy.wait_send()
    for k in range(groups):
        dest = dests[k]

        @pl.when(dest != group)
        def _():
            term_copy(k, dest, group).wait_send()

    run_all(*last)
    assert used <= SEMS


SEMS = 144


def finish_kernel(scale, hidden_ref, sums_ref, *outs):
    hidden_out, self_out, neigh_out, hb_out, cs_out, cn_out, cb_out, loss_out, lines = outs
    width = self_out.shape[0]
    hid = hidden_ref.shape[1]
    groups, rows = sums_ref.shape[:2]
    per = rows - width
    hidden_out[...] = hidden_ref[...]
    for n in range(groups):
        out = neigh_out if n % 2 else self_out
        at = n // 2 * hid
        out[:, at : at + hid] = sums_ref[n, 0:width, :]
        lines[n * per : n * per + per, :] = sums_ref[n, width:rows, :]
    classes = cs_out.shape[0]
    cs_out[...] = lines[0:classes, :]
    cn_out[...] = lines[160 : 160 + classes, :]
    hb_out[...] = lines[320:321, :]
    cb_out[:, 0:128] = lines[321:322, :]
    cb_out[:, 128:classes] = lines[322:323, 0 : classes - 128]
    loss_out[...] = lines[323:324, :] * scale


def body(
    node_features,
    target_nodes,
    first_hop,
    live_counts,
    seed_links,
    seed_labels,
    self_weight,
    neigh_weight,
    hidden_bias,
    class_self,
    class_neigh,
    class_bias,
):
    node_rows = node_features.shape[1]
    batches, targets = target_nodes.shape
    fan_one = first_hop.shape[1]
    seeds, fan_two = seed_links.shape[1:]
    hid = hidden_bias.shape[0]
    width, hidden_all = self_weight.shape
    classes = class_bias.shape[0]
    offset = (lax.axis_index("group") * node_rows).astype(jnp.int32)[None]
    parts = gather_rows(node_features, target_nodes, first_hop, offset).reshape(4, 4, 384, 128)
    f32, vmem = jnp.float32, pl.BlockSpec(memory_space=pltpu.VMEM)
    smem = pl.BlockSpec(memory_space=pltpu.SMEM)
    shapes = [
        ((4, 4, 384, 128), f32),
        ((4, 6, 4, 48, 128), f32),
        ((4, 6, 48, 128), f32),
        ((384, hidden_all), jnp.bfloat16),
        ((4, 2, targets, hid), f32),
        ((4, targets, hid), f32),
        ((2, 6, targets // 4, hid), f32),
        ((256, hid), f32),
        ((256, hid), f32),
        ((1, 256), f32),
        ((seeds, 256), jnp.int32),
        ((targets, 128), f32),
        ((seeds, 256), f32),
        ((seeds, 256), f32),
        ((4, seeds, 256), f32),
        ((4, 2, targets, hid), f32),
        ((16, width, 128), f32),
        ((16, width, 128), f32),
        ((16, 24, 128), f32),
        ((16, 24, 128), f32),
    ]
    hidden_layer, sums = pl.pallas_call(
        functools.partial(exchange_kernel, fan_one, fan_two),
        out_shape=(
            jax.ShapeDtypeStruct((targets, hid), jnp.bfloat16),
            jax.ShapeDtypeStruct((4, 4, width + 24, 128), f32),
        ),
        in_specs=[pl.BlockSpec(memory_space=pl.ANY)] + [vmem] * 6 + [smem, vmem, smem],
        out_specs=(vmem, vmem),
        scratch_shapes=[pltpu.VMEM(shape, kind) for shape, kind in shapes]
        + [
            pltpu.SemaphoreType.DMA,
            pltpu.SemaphoreType.DMA((SEMS,)),
            pltpu.SemaphoreType.DMA((SEMS,)),
        ],
        compiler_params=pltpu.CompilerParams(
            collective_id=0, has_side_effects=True, vmem_limit_bytes=48 * 1024 * 1024
        ),
        name="exchange",
    )(
        parts,
        self_weight,
        neigh_weight,
        hidden_bias[None],
        class_self.T,
        class_neigh.T,
        class_bias[None],
        live_counts,
        jnp.transpose(seed_links, (2, 0, 1)),
        seed_labels,
    )
    outs = pl.pallas_call(
        functools.partial(finish_kernel, 1.0 / (batches * seeds)),
        out_shape=(
            jax.ShapeDtypeStruct((targets, hid), jnp.bfloat16),
            jax.ShapeDtypeStruct((width, hidden_all), f32),
            jax.ShapeDtypeStruct((width, hidden_all), f32),
            jax.ShapeDtypeStruct((1, hid), f32),
            jax.ShapeDtypeStruct((classes, hid), f32),
            jax.ShapeDtypeStruct((classes, hid), f32),
            jax.ShapeDtypeStruct((1, classes), f32),
            jax.ShapeDtypeStruct((1, 128), f32),
        ),
        in_specs=[vmem] * 2,
        out_specs=(vmem,) * 8,
        scratch_shapes=[pltpu.VMEM((16 * 24, 128), f32)],
        name="finish",
    )(hidden_layer, sums.reshape(16, width + 24, 128))
    return (
        outs[0],
        outs[1],
        outs[2],
        outs[3][0],
        outs[4].T,
        outs[5].T,
        outs[6][0],
        outs[7][0, 0],
    )


def solution(mesh):
    in_specs = (
        P("mp", "group"),
        P(),
        P(),
        P("group"),
        P("group", None, None),
        P("group", None),
        P("mp", None),
        P("mp", None),
        P("mp"),
        P("mp", None),
        P("mp", None),
        P(),
    )
    out_specs = (
        P("group", "mp"),
        P("mp", None),
        P("mp", None),
        P("mp"),
        P("mp", None),
        P("mp", None),
        P(),
        P(),
    )
    return jax.shard_map(body, mesh=mesh, in_specs=in_specs, out_specs=out_specs, check_vma=False)
```

time: 164 us -> 118 us (0.72)
  Pallas kernels: 151 us -> 113 us
  local copies, waits for them, and re-layouts: 8.36 us -> 3.29 us
  between operations: 3.18 us -> 1.42 us
    pallas_call x1, Pallas kernels: 103 us -> 80.7 us  [body(): pl.pallas_call(functools.partial(exchange_kernel, fan_one, fan_two), out_...]
    pallas_call x1, Pallas kernels: 48.2 us -> 30.2 us  [gather_rows(): pl.pallas_call(gather_kernel, out_shape=jax.ShapeDtypeStruct((batches, 38...]
    pallas_call x0 -> x1, Pallas kernels: none -> 2.23 us  [body(): pl.pallas_call(functools.partial(finish_kernel, 1.0 / (batches * seeds)),...]
    unnamed x10 -> x24, local copies, waits for them, and re-layouts: 3.1 us -> 3.29 us
where the time goes in v2:
time: 118 us
  Pallas kernels  113 us (96%)
  local copies, waits for them, and re-layouts  3.29 us (3%)
  between operations  1.42 us (1%)
    pallas_call x1, Pallas kernels, body(): pl.pallas_call(functools.partial(exchange_kernel, fan_one, fan_two), out_...  80.7 us
    pallas_call x1, Pallas kernels, gather_rows(): pl.pallas_call(gather_kernel, out_shape=jax.ShapeDtypeStruct((batches, 38...  30.2 us
    unnamed x24, local copies, waits for them, and re-layouts  3.29 us

profile of v2, /device:TPU:0, one launch (start us, length us, event | category | flops | bytes accessed | tf_op | source)
XLA Modules:
  0.0 117.8 jit_solution(3378935810515331616)
XLA Ops:
  1.3 0.0 copy-start.1
  1.3 1.0 copy-done.1
  2.3 0.0 copy-start.7
  2.3 0.7 copy-done.7
  3.0 0.0 copy-start.2
  3.0 0.0 copy-start.3
  3.0 0.0 copy-start.8
  3.0 0.0 copy-start.9
  3.0 0.0 copy-start.10
  3.0 0.0 copy-start.11
  3.1 30.2 %gather_rows.1 = f32[16,384,128]{2,1,0:T(8,128)S(1)} custom-call(s32[1]{0:T(128)} %bitcast.offset_ref, bf16[96,16384]{1,0:T(8,128)(2,1)} %feat_ref.1, s32[16,256]{1,0:T(8,128)S(1)} %copy-done.7, s32[25,16,256]{2,1,0:T(8,128)S(1)} %bitcast.17), custom_call_target="tpu_custom_call" | custom-call | tf_op jit(solution)/shard_map/gather_rows/pallas_call | solution.py:171
  33.2 0.0 copy-done.2
  33.2 0.0 copy-done.3
  33.2 0.0 copy-done.5
  33.3 0.0 copy-done.6
  33.3 0.0 copy-done.8
  33.3 0.0 copy-done.9
  33.3 0.0 copy-done.10
  33.3 0.0 copy-done.11
  33.3 80.7 %exchange.1 = (bf16[256,128]{1,0:T(8,128)(2,1)S(1)}, f32[4,4,120,128]{3,2,1,0:T(8,128)S(1)}) custom-call(f32[4,4,384,128]{3,2,1,0:T(8,128)S(1)} %bitcast.15, bf16[96,1024]{1,0:T(8,128)(2,1)S(1)} %copy-done.2, bf16[96,1024]{1,0:T(8,128)(2,1)S(1)} %copy-done.3, f32[1,128]{1,0:T(1,128)S(1)} %bitcast.22, bf16[153,128]{1,0:T(8,128)(2,1)S(1)} %bitcast.18, ...), custom_call_target="tpu_custom_call" | custom-call | tf_op jit(solution)/shard_map/exchange/pallas_call | solution.py:764
  114.0 0.0 copy-start
  114.0 0.9 copy-done
  115.0 0.6 copy-done.4
  115.6 2.2 %finish.1 = (bf16[256,128]{1,0:T(8,128)(2,1)}, f32[96,1024]{1,0:T(8,128)}, f32[96,1024]{1,0:T(8,128)}, f32[1,128]{1,0:T(1,128)}, f32[153,128]{1,0:T(8,128)}, /*i...) custom-call(bf16[256,128]{1,0:T(8,128)(2,1)} %copy-done.4, f32[16,120,128]{2,1,0:T(8,128)} %bitcast.16), custom_call_target="tpu_custom_call" | custom-call | tf_op jit(solution)/shard_map/finish/pallas_call | solution.py:794
  (3 shorter events, 0.0 us)
Async XLA Ops:
  1.3 1.0 copy-start.1
  2.3 0.7 copy-start.7
  3.0 30.2 %copy-start.2 = (bf16[96,1024]{1,0:T(8,128)(2,1)S(1)}, bf16[96,1024]{1,0:T(8,128)(2,1)}, u32[]{:S(2)}) copy-start(bf16[96,1024]{1,0:T(8,128)(2,1)} %ws_ref.1) | copy-start | bytes 589828
  3.0 30.2 %copy-start.3 = (bf16[96,1024]{1,0:T(8,128)(2,1)S(1)}, bf16[96,1024]{1,0:T(8,128)(2,1)}, u32[]{:S(2)}) copy-start(bf16[96,1024]{1,0:T(8,128)(2,1)} %wn_ref.1) | copy-start | bytes 589828
  3.0 30.2 %copy-start.5 = (bf16[128,153]{0,1:T(8,128)(2,1)S(1)}, bf16[128,153]{0,1:T(8,128)(2,1)}, u32[]{:S(2)}) copy-start(bf16[128,153]{0,1:T(8,128)(2,1)} %param.21) | copy-start | bytes 117508
  3.0 30.2 %copy-start.6 = (bf16[128,153]{0,1:T(8,128)(2,1)S(1)}, bf16[128,153]{0,1:T(8,128)(2,1)}, u32[]{:S(2)}) copy-start(bf16[128,153]{0,1:T(8,128)(2,1)} %param.22) | copy-start | bytes 117508
  3.0 30.2 %copy-start.8 = (s32[1,32,15]{1,0,2:T(1,128)S(1)}, s32[1,32,15]{1,0,2:T(1,128)}, u32[]{:S(2)}) copy-start(s32[1,32,15]{1,0,2:T(1,128)} %param.16) | copy-start | bytes 5764
  3.0 30.2 %copy-start.9 = (f32[153]{0:T(256)S(1)}, f32[153]{0:T(256)}, u32[]{:S(2)}) copy-start(f32[153]{0:T(256)} %param.23) | copy-start | bytes 1840
  3.0 30.2 %copy-start.10 = (f32[128]{0:T(128)S(1)}, f32[128]{0:T(128)}, u32[]{:S(2)}) copy-start(f32[128]{0:T(128)} %param.20) | copy-start | bytes 1540
  3.0 30.2 %copy-start.11 = (s32[1,32]{1,0:T(1,128)S(1)}, s32[1,32]{1,0:T(1,128)}, u32[]{:S(2)}) copy-start(s32[1,32]{1,0:T(1,128)} %labels_ref.1) | copy-start | bytes 388
  114.0 0.9 copy-start
  115.0 0.6 copy-start.4

commit v3 on v2

--- a/solution.py
+++ b/solution.py
@@ -12,7 +12,13 @@
 TURNS = 18
 
 
-def gather_kernel(offset_ref, feat_ref, targets_ref, hops_ref, out_ref, table, acc, ids, codes, counts, first_s, counts_s, extra_s, sems):
+def gather_kernel(offset_ref, feat_hbm, targets_hbm, hops_hbm, out_ref, feat_ref, targets_ref, hops_ref, table, acc, ids, codes, counts, first_s, counts_s, extra_s, sems, load_sems):
+    loads = [
+        pltpu.make_async_copy(src, dst, load_sems.at[n])
+        for n, (src, dst) in enumerate(((hops_hbm, hops_ref), (targets_hbm, targets_ref), (feat_hbm, feat_ref)))
+    ]
+    for load in loads:
+        load.start()
     width, nodes = feat_ref.shape
     lists, rows = ids.shape[:2]
     fan, batches, targets = hops_ref.shape
@@ -20,6 +26,8 @@
     half = rows * 128
     slots = 2 * half
     cols = targets // 128
+    loads[0].wait()
+    loads[1].wait()
     for n in range(cols):
         at, wide = pl.ds(n * batches, batches), slice(n * 128, n * 128 + 128)
         ids[0:fan, at] = hops_ref[:, :, wide] - offset_ref[0]
@@ -78,6 +86,7 @@
             turn(q * TURNS + n)
         return carry
 
+    loads[2].wait()
     lax.fori_loop(0, lists // BLOCK, compact, 0)
     copy_counts = pltpu.make_async_copy(counts, counts_s, sems.at[0])
     copy_counts.start()
@@ -147,16 +156,18 @@
 
     lax.fori_loop(0, used, rest, 0)
 
-    lanes = lax.broadcasted_iota(jnp.int32, (64, 128), 1)
+    lanes = lax.broadcasted_iota(jnp.int32, (32, 128), 1)
 
     def pack(i, carry):
         for s in range(2):
-            base = (1 - s) * half + i * 256
-            a, b, c, d = [acc[pl.ds(pl.multiple_of(base + n * 64, 64), 64), :] for n in range(4)]
-            b, c, d = pltpu.roll(b, 96, 1), pltpu.roll(c, 64, 1), pltpu.roll(d, 32, 1)
-            out_ref[i, pl.ds(s * 192, 64), :] = jnp.where(lanes < 96, a, b)
-            out_ref[i, pl.ds(s * 192 + 64, 64), :] = jnp.where(lanes < 64, b, c)
-            out_ref[i, pl.ds(s * 192 + 128, 64), :] = jnp.where(lanes < 32, c, d)
+            for n in range(2):
+                base = (1 - s) * half + i * 256 + n * 128
+                a, b, c, d = [acc[pl.ds(pl.multiple_of(base + k * 32, 32), 32), :] for k in range(4)]
+                b, c, d = pltpu.roll(b, 96, 1), pltpu.roll(c, 64, 1), pltpu.roll(d, 32, 1)
+                row = s * 192 + n * 96
+                out_ref[i, pl.ds(row, 32), :] = jnp.where(lanes < 96, a, b)
+                out_ref[i, pl.ds(row + 32, 32), :] = jnp.where(lanes < 64, b, c)
+                out_ref[i, pl.ds(row + 64, 32), :] = jnp.where(lanes < 32, c, d)
         return carry
 
     lax.fori_loop(0, half // 256, pack, 0)
@@ -167,13 +178,17 @@
     batches, targets = target_nodes.shape
     rows = batches * targets // 128
     lists = 28
-    vmem = pl.BlockSpec(memory_space=pltpu.VMEM)
+    hbm = pl.BlockSpec(memory_space=pltpu.HBM)
+    hops = jnp.moveaxis(first_hop, 1, 0)
     return pl.pallas_call(
         gather_kernel,
         out_shape=jax.ShapeDtypeStruct((batches, 384, 128), jnp.float32),
-        in_specs=[pl.BlockSpec(memory_space=pltpu.SMEM)] + [vmem] * 3,
-        out_specs=vmem,
+        in_specs=[pl.BlockSpec(memory_space=pltpu.SMEM)] + [hbm] * 3,
+        out_specs=pl.BlockSpec(memory_space=pltpu.VMEM),
         scratch_shapes=[
+            pltpu.VMEM(features.shape, features.dtype),
+            pltpu.VMEM(target_nodes.shape, jnp.int32),
+            pltpu.VMEM(hops.shape, jnp.int32),
             pltpu.VMEM((nodes + 8, 128), jnp.float32),
             pltpu.VMEM((batches * 512 + 8, 128), jnp.float32),
             pltpu.VMEM((lists, rows, 128), jnp.int32),
@@ -183,10 +198,11 @@
             pltpu.SMEM((lists + 4, 128), jnp.int32),
             pltpu.SMEM((128,), jnp.int32),
             pltpu.SemaphoreType.DMA((lists * TOP + 2,)),
+            pltpu.SemaphoreType.DMA((3,)),
         ],
         compiler_params=pltpu.CompilerParams(vmem_limit_bytes=48 * 1024 * 1024),
         name="gather_rows",
-    )(offset, features, target_nodes, jnp.moveaxis(first_hop, 1, 0))
+    )(offset, features, target_nodes, hops)
 
 
 MESH = pl.DeviceIdType.MESH
@@ -246,7 +262,7 @@
 
 
 def grid_sum(buf, spans, in_wide, in_thin, ssem, rsem, base, x, y, xs, ys):
-    def route(n, h, lo, half):
+    def route(h, n, lo, half):
         def wide(d, p):
             at = pl.ds(lo + p * half, half)
             return buf.at[d, :, at] if h == 0 else buf.at[:, d, at]
@@ -259,7 +275,18 @@
         yield from ring_sum(wide, lambda k: in_wide.at[n, k], ssem, rsem, base + n * 12, *first)
         yield from ring_sum(thin, lambda k: in_thin.at[n, k], ssem, rsem, base + n * 12 + 6, *second)
 
-    return [route(n, *span) for n, span in enumerate(spans)]
+    return [route(*span) for span in spans]
+
+
+def together(routes):
+    active = list(routes)
+    while active:
+        for route in list(active):
+            try:
+                next(route)
+            except StopIteration:
+                active.remove(route)
+        yield
 
 
 def grid_gather(buf, spans, ssem, rsem, base, x, y, device):
@@ -307,12 +334,13 @@
     return [route(n, *span) for n, span in enumerate(spans)]
 
 
-def unpack(ref, x, y, row, lane64):
-    p = [ref[x, y, pl.ds(row + 64 * n, 64), :] for n in range(3)]
-    b = jnp.where(lane64 < 32, pltpu.roll(p[0], 32, 1), pltpu.roll(p[1], 32, 1))
-    c = jnp.where(lane64 < 64, pltpu.roll(p[1], 64, 1), pltpu.roll(p[2], 64, 1))
+def unpack(ref, x, y, row):
+    lane = lax.broadcasted_iota(jnp.int32, (32, 128), 1)
+    p = [ref[x, y, pl.ds(row + 32 * n, 32), :] for n in range(3)]
+    b = jnp.where(lane < 32, pltpu.roll(p[0], 32, 1), pltpu.roll(p[1], 32, 1))
+    c = jnp.where(lane < 64, pltpu.roll(p[1], 64, 1), pltpu.roll(p[2], 64, 1))
     d = pltpu.roll(p[2], 96, 1)
-    out = [jnp.where(lane64 < 96, v, 0.0) for v in (p[0], b, c, d)]
+    out = [jnp.where(lane < 96, v, 0.0) for v in (p[0], b, c, d)]
     return jnp.concatenate(out, axis=0)
 
 
@@ -351,8 +379,9 @@
     pre_parts,
     in_core,
     in_z,
-    cs_pad,
-    cn_pad,
+    classes_all,
+    self_all,
+    neigh_all,
     cb_pad,
     label_rows,
     link_pad,
@@ -399,51 +428,6 @@
     pl.semaphore_wait(barrier, len(nears))
     load.wait()
 
-    used = 0
-    spans = ((0, 0, 48), (1, 192, 48), (0, 96, 48), (1, 288, 48))
-    rows_sum = grid_sum(parts, spans, in_wide, in_thin, ssem, rsem, used, x, y, xs, ys)
-    used += 48
-    for route in rows_sum:
-        next(route)
-
-    width = ws_ref.shape[0]
-    targets, hid = hidden_ref.shape
-    seeds = labels_ref.shape[1]
-    classes = cs_ref.shape[0]
-    weights[...] = jnp.zeros_like(weights)
-    weights[0:width, :] = ws_ref[...]
-    weights[128 : 128 + width, :] = wn_ref[...]
-    weights[256 : 256 + width, :] = wn_ref[...]
-    cs_pad[...] = jnp.zeros_like(cs_pad)
-    cn_pad[...] = jnp.zeros_like(cn_pad)
-    cb_pad[...] = jnp.zeros_like(cb_pad)
-    cs_pad[0:classes, :] = cs_ref[...].astype(jnp.float32)
-    cn_pad[0:classes, :] = cn_ref[...].astype(jnp.float32)
-    cb_pad[:, 0:classes] = cb_ref[...]
-    extras[...] = jnp.zeros_like(extras)
-    for s in range(seeds):
-        label_rows[s : s + 1, :] = jnp.full((1, 256), labels_ref[0, s], jnp.int32)
-    seed_cols = lax.broadcasted_iota(jnp.int32, (targets, seeds), 0)
-    counted = jnp.zeros((targets, seeds), jnp.float32)
-    for k in range(fan_two):
-        counted = counted + jnp.where(seed_cols == links_ref[k], 1.0, 0.0)
-    link_pad[...] = jnp.zeros_like(link_pad)
-    link_pad[:, 0:seeds] = counted
-    links_t = link_pad[...]
-    links_f = links_t.T[0:seeds]
-    run_all(*rows_sum)
-
-    lane64 = lax.broadcasted_iota(jnp.int32, (64, 128), 1)
-    target_rows = lax.broadcasted_iota(jnp.int32, (targets, 128), 0)
-    self_rows = unpack(parts, x, y, 0, lane64)
-    neigh_rows = unpack(parts, x, y, 192, lane64) / fan_one
-    neigh_hi, neigh_lo = split(neigh_rows)
-    left_side = jnp.concatenate([self_rows.astype(jnp.bfloat16), neigh_hi, neigh_lo], axis=1)
-
-    def block_of(zz, cc):
-        at = pl.multiple_of((zz * 2 + cc) * hid, hid)
-        pre_parts[zz, cc] = dot(left_side, weights[:, pl.ds(at, hid)])
-
     def core_copy(src, dst, k):
         return pltpu.make_async_remote_copy(
             src_ref=src,
@@ -454,12 +438,70 @@
             device_id_type=MESH,
         )
 
+    def spread(ref_of, base):
+        started = []
+        for k, (slot, near) in enumerate(((1, zs[0]), (3, zs[1]), (2, opposite))):
+            started.append(
+                pltpu.make_async_remote_copy(
+                    src_ref=ref_of(0, 0),
+                    dst_ref=ref_of(slot, 0),
+                    send_sem=ssem.at[base + k],
+                    recv_sem=rsem.at[base + k],
+                    device_id=near,
+                    device_id_type=MESH,
+                )
+            )
+        started.append(core_copy(ref_of(0, 0), ref_of(0, 1), base + 3))
+        for copy in started:
+            copy.start()
+        yield (0, 0)
+        started[3].wait_recv()
+        yield (0, 1)
+        for k, slot in enumerate((1, 3)):
+            started[k].wait_recv()
+            started.append(core_copy(ref_of(slot, 0), ref_of(slot, 1), base + 3 + slot))
+            started[-1].start()
+            yield (slot, 0)
+        for k, slot in enumerate((1, 3)):
+            started[4 + k].wait_recv()
+            yield (slot, 1)
+        started[2].wait_recv()
+        started.append(core_copy(ref_of(2, 0), ref_of(2, 1), base + 5))
+        started[-1].start()
+        yield (2, 0)
+        started[6].wait_recv()
+        yield (2, 1)
+        for copy in started:
+            copy.wait_send()
+
+    used = 0
+    width = ws_ref.shape[0]
+    targets, hid = hidden_ref.shape
     half_rows = targets // 2
-
-    def owner_sum(n, base):
+    seeds = labels_ref.shape[1]
+    classes = cs_ref.shape[0]
+
+    def half_route(n, base):
+        spans = ((0, 2 * n, n * 96, 48), (1, 2 * n + 1, 192 + n * 96, 48))
+        yield from together(grid_sum(parts, spans, in_wide, in_thin, ssem, rsem, 0, x, y, xs, ys))
         at = pl.ds(n * half_rows, half_rows)
+        own_self = unpack(parts, x, y, n * 96)
+        own_neigh = unpack(parts, x, y, 192 + n * 96) / fan_one
+        self_all[at, :] = own_self
+        neigh_all[at, :] = own_neigh
+        neigh_hi, neigh_lo = split(own_neigh)
+        left_side = jnp.concatenate([own_self.astype(jnp.bfloat16), neigh_hi, neigh_lo], axis=1)
+
+        def block_of(zz, cc):
+            cols = pl.multiple_of((zz * 2 + cc) * hid, hid)
+            pre_parts[zz, cc, at] = dot(left_side, weights[:, pl.ds(cols, hid)])
+
+        for zz in range(4):
+            block_of(zz, 1 - core)
         copy = core_copy(pre_parts.at[:, 1 - core, at], in_core.at[:, at], base)
         copy.start()
+        for zz in range(4):
+            block_of(zz, core)
         yield
         copy.wait()
         for zz in range(4):
@@ -475,29 +517,63 @@
             *zs,
         )
 
-    for zz in range(4):
-        block_of(zz, 1 - core)
-    owners = [owner_sum(n, used + 7 * n) for n in range(2)]
+    used += 48
+    owners = [half_route(n, used + 7 * n) for n in range(2)]
     used += 14
-    for route in owners:
-        next(route)
-    for zz in range(4):
-        block_of(zz, core)
-    self_t = self_rows.T[0:width]
-    neigh_t = neigh_rows.T[0:width]
-    neigh_t_hi, neigh_t_lo = split(neigh_t)
-    rows_hi = jnp.concatenate([self_t.astype(jnp.bfloat16), neigh_t_hi], axis=0)
-    run_all(*owners)
+    next(owners[0])
+
+    sent = 160
+    for n in range(4):
+        for a in range(2):
+            for kind in range(2):
+                classes_all[n, a, kind, sent:256, :] = jnp.zeros((256 - sent, hid), jnp.float32)
+    for kind in range(2):
+        classes_all[0, 0, kind, 0:sent, :] = jnp.zeros((sent, hid), jnp.float32)
+    classes_all[0, 0, 0, 0:classes, :] = cs_ref[...].astype(jnp.float32)
+    classes_all[0, 0, 1, 0:classes, :] = cn_ref[...].astype(jnp.float32)
+    class_spread = spread(lambda n, a: classes_all.at[n, a, :, pl.ds(0, sent)], used)
+    used += 7
+    next(class_spread)
+    weights[...] = jnp.zeros_like(weights)
+    weights[0:width, :] = ws_ref[...]
+    weights[128 : 128 + width, :] = wn_ref[...]
+    weights[256 : 256 + width, :] = wn_ref[...]
+    next(owners[0])
+    next(owners[1])
+    cb_pad[...] = jnp.zeros_like(cb_pad)
+    cb_pad[:, 0:classes] = cb_ref[...]
+    extras[...] = jnp.zeros_like(extras)
+    for s in range(seeds):
+        label_rows[s : s + 1, :] = jnp.full((1, 256), labels_ref[0, s], jnp.int32)
+    seed_cols = lax.broadcasted_iota(jnp.int32, (targets, seeds), 0)
+    counted = jnp.zeros((targets, seeds), jnp.float32)
+    for k in range(fan_two):
+        counted = counted + jnp.where(seed_cols == links_ref[k], 1.0, 0.0)
+    link_pad[...] = jnp.zeros_like(link_pad)
+    link_pad[:, 0:seeds] = counted
+    links_t = link_pad[...]
+    links_f = links_t.T[0:seeds].astype(jnp.bfloat16)
+    links_b = links_t.astype(jnp.bfloat16)
+    target_rows = lax.broadcasted_iota(jnp.int32, (targets, 128), 0)
+
+    def later(route, rounds):
+        for _ in range(rounds):
+            yield
+        yield from route
+
+    run_all(*owners, later(class_spread, 4))
 
     pre = pre_parts[z, core] + hb_ref[...]
+    piece[0, 0] = pre
     alive = (target_rows < live_ref[0]) & (pre > 0.0)
     hidden = jnp.where(alive, pre, 0.0).astype(jnp.bfloat16)
     hidden_ref[...] = hidden
     active = hidden.astype(jnp.float32)
     seed_self = active[0:seeds]
-    seed_neigh = dot(links_f.astype(jnp.bfloat16), hidden) / fan_two
+    seed_neigh = dot(links_f, hidden) / fan_two
     rows_cols = ((1,), (1,))
-    logit_own[...] = high_dot(seed_self, cs_pad[...], rows_cols) + high_dot(seed_neigh, cn_pad[...], rows_cols)
+    own_self = high_dot(seed_self, classes_all[0, 0, 0], rows_cols)
+    logit_own[...] = own_self + high_dot(seed_neigh, classes_all[0, 0, 1], rows_cols)
     to_core = core_copy(logit_own, logit_core, used)
     used += 1
     to_core.start()
@@ -522,6 +598,12 @@
 
     sends = z_sends(logit_z.at[z], used)
     used += 3
+    pre_spread = spread(lambda n, a: piece.at[n, a], used)
+    used += 7
+    next(pre_spread)
+    self_t = self_all[...].T[0:width].astype(jnp.bfloat16)
+    neigh_t_hi, neigh_t_lo = split(neigh_all[...].T[0:width])
+    rows_hi = jnp.concatenate([self_t, neigh_t_hi], axis=0)
     for c in sends:
         c.wait()
     logits = (logit_z[0] + logit_z[1]) + (logit_z[2] + logit_z[3]) + cb_pad[...]
@@ -532,36 +614,63 @@
     onehot = jnp.where(lanes == label_rows[...], 1.0, 0.0)
     losses = log_total - jnp.sum(onehot * logits, axis=1, keepdims=True)
     dlogit = jnp.exp(logits - log_total) - onehot
-    back_self = high_dot(dlogit, cs_pad[...])
-    back_neigh = high_dot(dlogit, cn_pad[...]) / fan_two
-    back_neigh = jnp.concatenate([back_neigh, jnp.zeros((128 - seeds, hid), jnp.float32)], axis=0)
-    grad_act = high_dot(links_t, back_neigh)
-    grad_act = grad_act + jnp.concatenate(
-        [back_self, jnp.zeros((targets - seeds, hid), jnp.float32)], axis=0
-    )
-    grad_pre = jnp.where(alive, grad_act, 0.0)
-    piece[0, 0] = grad_pre
-
-    def piece_send(slot, target, k):
-        copy = pltpu.make_async_remote_copy(
-            src_ref=piece.at[0, 0],
-            dst_ref=piece.at[slot, 0],
-            send_sem=ssem.at[used + k],
-            recv_sem=rsem.at[used + k],
-            device_id=target,
+    dlogit_hi, dlogit_lo = split(dlogit)
+
+    def back(n, across, kind):
+        side = classes_all[n, across, kind].astype(jnp.bfloat16)
+        return dot(dlogit_hi, side) + dot(dlogit_lo, side)
+
+    def grad_of(n, across):
+        low = jnp.zeros((128 - seeds, hid), jnp.float32)
+        neigh_hi, neigh_lo = split(jnp.concatenate([back(n, across, 1) / fan_two, low], axis=0))
+        top_rows = jnp.concatenate([back(n, across, 0), jnp.zeros((targets - seeds, hid), jnp.float32)], axis=0)
+        act = dot(links_b, neigh_hi) + dot(links_b, neigh_lo) + top_rows
+        on = (target_rows < live_ref[0]) & (piece[n, across] > 0.0)
+        return jnp.where(on, act, 0.0)
+
+    term_base = used
+    used += groups
+
+    def term_copy(k, dest, k_recv):
+        return pltpu.make_async_remote_copy(
+            src_ref=terms.at[k],
+            dst_ref=in_terms.at[group],
+            send_sem=ssem.at[term_base + k],
+            recv_sem=rsem.at[term_base + k_recv],
+            device_id=(dest, m),
             device_id_type=MESH,
         )
-        copy.start()
-        return copy
-
-    spread = [piece_send(1, zs[0], 0), piece_send(3, zs[1], 1), piece_send(2, opposite, 2)]
-    used += 3
-    core_base = used
-    used += 4
-    to_sibling = [core_copy(piece.at[0, 0], piece.at[0, 1], core_base)]
-    to_sibling[0].start()
-
-    dlogit_t = dlogit.T[0:160]
+
+    dests = {}
+
+    hidden_line = []
+
+    def block_terms(step, n, across):
+        zz = lax.rem(z + 4 - n, 4)
+        cc = 1 - core if across else core
+        grad_pre = grad_of(n, across)
+        if step == 0:
+            hidden_line.append(jnp.sum(grad_pre, axis=0, keepdims=True))
+        g_hi, g_lo = split(grad_pre)
+        term = dot(rows_hi, g_hi) + dot(rows_hi, g_lo)
+        terms[2 * step] = term[0:width]
+        terms[2 * step + 1] = term[width : 2 * width] + dot(neigh_t_lo, g_hi)
+        for s in range(2):
+            k = 2 * step + s
+            dests[k] = dest = zz * 4 + cc * 2 + s
+
+            @pl.when(dest != group)
+            def _():
+                term_copy(k, dest, group).start()
+
+            @pl.when(dest == group)
+            def _():
+                in_terms[group] = terms[k]
+
+    block_terms(0, 0, 0)
+    block_terms(1, *next(pre_spread))
+
+    dlogit_t = dlogit.T[0:sent]
     class_grads = jnp.concatenate(
         [high_dot(dlogit_t, seed_self), high_dot(dlogit_t, seed_neigh)], axis=0
     )
@@ -570,7 +679,7 @@
         extras[n // per, n % per : n % per + 8] = class_grads[n : n + 8]
     row_sum = jnp.sum(dlogit, axis=0, keepdims=True)
     lines = (
-        jnp.sum(grad_pre, axis=0, keepdims=True),
+        hidden_line[0],
         row_sum[:, 0:128],
         row_sum[:, 128:256],
         jnp.broadcast_to(jnp.sum(losses, axis=0, keepdims=True), (1, 128)),
@@ -591,63 +700,9 @@
         extra_sends.append(copy)
     used += groups - 1
 
-    term_base = used
-    used += groups
-
-    def term_copy(k, dest, k_recv):
-        return pltpu.make_async_remote_copy(
-            src_ref=terms.at[k],
-            dst_ref=in_terms.at[group],
-            send_sem=ssem.at[term_base + k],
-            recv_sem=rsem.at[term_base + k_recv],
-            device_id=(dest, m),
-            device_id_type=MESH,
-        )
-
-    dests = {}
-
-    def block_terms(step, n, across):
-        zz = lax.rem(z + 4 - n, 4)
-        cc = 1 - core if across else core
-        g_hi, g_lo = split(piece[n, across])
-        term = dot(rows_hi, g_hi) + dot(rows_hi, g_lo)
-        terms[2 * step] = term[0:width]
-        terms[2 * step + 1] = term[width : 2 * width] + dot(neigh_t_lo, g_hi)
-        for s in range(2):
-            k = 2 * step + s
-            dests[k] = dest = zz * 4 + cc * 2 + s
-
-            @pl.when(dest != group)
-            def _():
-                term_copy(k, dest, group).start()
-
-            @pl.when(dest == group)
-            def _():
-                in_terms[group] = terms[k]
-
-    def forward(n):
-        copy = core_copy(piece.at[n, 0], piece.at[n, 1], core_base + n)
-        copy.start()
-        to_sibling.append(copy)
-
-    block_terms(0, 0, 0)
-    to_sibling[0].wait_recv()
-    block_terms(1, 0, 1)
-    spread[0].wait_recv()
-    forward(1)
-    block_terms(2, 1, 0)
-    spread[1].wait_recv()
-    forward(3)
-    block_terms(3, 3, 0)
-    to_sibling[1].wait_recv()
-    block_terms(4, 1, 1)
-    to_sibling[2].wait_recv()
-    block_terms(5, 3, 1)
-    spread[2].wait_recv()
-    forward(2)
-    block_terms(6, 2, 0)
-    to_sibling[3].wait_recv()
-    block_terms(7, 2, 1)
+    for step in range(2, groups // 2):
+        block_terms(step, *next(pre_spread))
+    run_all(pre_spread)
 
     for copy in extra_sends:
         copy.wait_recv()
@@ -677,7 +732,7 @@
     used += 30
     for route in last:
         next(route)
-    for copy in spread + to_sibling + extra_sends:
+    for copy in extra_sends:
         copy.wait_send()
     for k in range(groups):
         dest = dests[k]
@@ -690,7 +745,7 @@
     assert used <= SEMS
 
 
-SEMS = 144
+SEMS = 160
 
 
 def finish_kernel(scale, hidden_ref, sums_ref, *outs):
@@ -747,8 +802,9 @@
         ((4, 2, targets, hid), f32),
         ((4, targets, hid), f32),
         ((2, 6, targets // 4, hid), f32),
-        ((256, hid), f32),
-        ((256, hid), f32),
+        ((4, 2, 2, 256, hid), f32),
+        ((targets, 128), f32),
+        ((targets, 128), f32),
         ((1, 256), f32),
         ((seeds, 256), jnp.int32),
         ((targets, 128), f32),

time: 118 us -> 119 us (level)
  no operation moved by 1% of the time
where the time goes in v3:
time: 119 us
  Pallas kernels  114 us (96%)
  local copies, waits for them, and re-layouts  3.29 us (3%)
  between operations  1.42 us (1%)
    pallas_call x1, Pallas kernels, body(): pl.pallas_call(functools.partial(exchange_kernel, fan_one, fan_two), out_...  81.6 us
    pallas_call x1, Pallas kernels, gather_rows(): pl.pallas_call(gather_kernel, out_shape=jax.ShapeDtypeStruct((batches, 38...  30.1 us
    unnamed x24, local copies, waits for them, and re-layouts  3.29 us

profile of v3, /device:TPU:0, one launch (start us, length us, event | category | flops | bytes accessed | tf_op | source)
XLA Modules:
  0.0 118.6 jit_solution(11216882581078563876)
XLA Ops:
  1.3 0.0 copy-start.1
  1.3 1.0 copy-done.1
  2.3 0.0 copy-start.7
  2.3 0.7 copy-done.7
  3.0 0.0 copy-start.2
  3.0 0.0 copy-start.3
  3.0 0.0 copy-start.8
  3.0 0.0 copy-start.9
  3.0 0.0 copy-start.10
  3.0 0.0 copy-start.11
  3.1 30.1 %gather_rows.1 = f32[16,384,128]{2,1,0:T(8,128)S(1)} custom-call(s32[1]{0:T(128)} %bitcast.offset_ref, bf16[96,16384]{1,0:T(8,128)(2,1)} %feat_hbm.1, s32[16,256]{1,0:T(8,128)S(1)} %copy-done.7, s32[25,16,256]{2,1,0:T(8,128)S(1)} %bitcast.17), custom_call_target="tpu_custom_call" | custom-call | tf_op jit(solution)/shard_map/gather_rows/pallas_call | solution.py:183
  33.1 0.0 copy-done.2
  33.1 0.0 copy-done.3
  33.2 0.0 copy-done.5
  33.2 0.0 copy-done.6
  33.2 0.0 copy-done.8
  33.2 0.0 copy-done.9
  33.2 0.0 copy-done.10
  33.2 0.0 copy-done.11
  33.2 81.6 %exchange.1 = (bf16[256,128]{1,0:T(8,128)(2,1)S(1)}, f32[4,4,120,128]{3,2,1,0:T(8,128)S(1)}) custom-call(f32[4,4,384,128]{3,2,1,0:T(8,128)S(1)} %bitcast.15, bf16[96,1024]{1,0:T(8,128)(2,1)S(1)} %copy-done.2, bf16[96,1024]{1,0:T(8,128)(2,1)S(1)} %copy-done.3, f32[1,128]{1,0:T(1,128)S(1)} %bitcast.22, bf16[153,128]{1,0:T(8,128)(2,1)S(1)} %bitcast.18, ...), custom_call_target="tpu_custom_call" | custom-call | tf_op jit(solution)/shard_map/exchange/pallas_call | solution.py:820
  114.8 0.0 copy-start
  114.8 0.9 copy-done
  115.7 0.6 copy-done.4
  116.4 2.2 %finish.1 = (bf16[256,128]{1,0:T(8,128)(2,1)}, f32[96,1024]{1,0:T(8,128)}, f32[96,1024]{1,0:T(8,128)}, f32[1,128]{1,0:T(1,128)}, f32[153,128]{1,0:T(8,128)}, /*i...) custom-call(bf16[256,128]{1,0:T(8,128)(2,1)} %copy-done.4, f32[16,120,128]{2,1,0:T(8,128)} %bitcast.16), custom_call_target="tpu_custom_call" | custom-call | tf_op jit(solution)/shard_map/finish/pallas_call | solution.py:850
  (3 shorter events, 0.0 us)
Async XLA Ops:
  1.3 1.0 copy-start.1
  2.3 0.7 copy-start.7
  3.0 30.1 %copy-start.2 = (bf16[96,1024]{1,0:T(8,128)(2,1)S(1)}, bf16[96,1024]{1,0:T(8,128)(2,1)}, u32[]{:S(2)}) copy-start(bf16[96,1024]{1,0:T(8,128)(2,1)} %ws_ref.1) | copy-start | bytes 589828
  3.0 30.1 %copy-start.3 = (bf16[96,1024]{1,0:T(8,128)(2,1)S(1)}, bf16[96,1024]{1,0:T(8,128)(2,1)}, u32[]{:S(2)}) copy-start(bf16[96,1024]{1,0:T(8,128)(2,1)} %wn_ref.1) | copy-start | bytes 589828
  3.0 30.1 %copy-start.5 = (bf16[128,153]{0,1:T(8,128)(2,1)S(1)}, bf16[128,153]{0,1:T(8,128)(2,1)}, u32[]{:S(2)}) copy-start(bf16[128,153]{0,1:T(8,128)(2,1)} %param.21) | copy-start | bytes 117508
  3.0 30.2 %copy-start.6 = (bf16[128,153]{0,1:T(8,128)(2,1)S(1)}, bf16[128,153]{0,1:T(8,128)(2,1)}, u32[]{:S(2)}) copy-start(bf16[128,153]{0,1:T(8,128)(2,1)} %param.22) | copy-start | bytes 117508
  3.0 30.2 %copy-start.8 = (s32[1,32,15]{1,0,2:T(1,128)S(1)}, s32[1,32,15]{1,0,2:T(1,128)}, u32[]{:S(2)}) copy-start(s32[1,32,15]{1,0,2:T(1,128)} %param.16) | copy-start | bytes 5764
  3.0 30.2 %copy-start.9 = (f32[153]{0:T(256)S(1)}, f32[153]{0:T(256)}, u32[]{:S(2)}) copy-start(f32[153]{0:T(256)} %param.23) | copy-start | bytes 1840
  3.0 30.2 %copy-start.10 = (f32[128]{0:T(128)S(1)}, f32[128]{0:T(128)}, u32[]{:S(2)}) copy-start(f32[128]{0:T(128)} %param.20) | copy-start | bytes 1540
  3.0 30.2 %copy-start.11 = (s32[1,32]{1,0:T(1,128)S(1)}, s32[1,32]{1,0:T(1,128)}, u32[]{:S(2)}) copy-start(s32[1,32]{1,0:T(1,128)} %labels_ref.1) | copy-start | bytes 388
  114.8 0.9 copy-start
  115.7 0.6 copy-start.4

commit v4 on v3

--- a/solution.py
+++ b/solution.py
@@ -261,19 +261,38 @@
         c.wait_send()
 
 
-def grid_sum(buf, spans, in_wide, in_thin, ssem, rsem, base, x, y, xs, ys):
+def grid_sum(buf, spans, in_wide, in_thin, ssem, rsem, base, x, y, xs, ys, device):
     def route(h, n, lo, half):
         def wide(d, p):
             at = pl.ds(lo + p * half, half)
             return buf.at[d, :, at] if h == 0 else buf.at[:, d, at]
 
-        def thin(d, p):
-            at = pl.ds(lo + p * half, half)
+        def thin(d):
+            at = pl.ds(lo, 2 * half)
             return buf.at[x, d, at] if h == 0 else buf.at[d, y, at]
 
-        first, second = ((x,) + xs, (y,) + ys) if h == 0 else ((y,) + ys, (x,) + xs)
-        yield from ring_sum(wide, lambda k: in_wide.at[n, k], ssem, rsem, base + n * 12, *first)
-        yield from ring_sum(thin, lambda k: in_thin.at[n, k], ssem, rsem, base + n * 12 + 6, *second)
+        first = (x,) + xs if h == 0 else (y,) + ys
+        yield from ring_sum(wide, lambda k: in_wide.at[n, k], ssem, rsem, base + n * 9, *first)
+        i = y if h == 0 else x
+        copies = []
+        for k, step in enumerate((1, 3, 2)):
+            copies.append(
+                pltpu.make_async_remote_copy(
+                    src_ref=thin(lax.rem(i + step, 4)),
+                    dst_ref=in_thin.at[n, k],
+                    send_sem=ssem.at[base + n * 9 + 6 + k],
+                    recv_sem=rsem.at[base + n * 9 + 6 + k],
+                    device_id=device(0, step) if h == 0 else device(step, 0),
+                    device_id_type=MESH,
+                )
+            )
+            copies[-1].start()
+        yield
+        for k, copy in enumerate(copies):
+            copy.wait_recv()
+            thin(i)[...] = thin(i)[...] + in_thin[n, k]
+        for copy in copies:
+            copy.wait_send()
 
     return [route(*span) for span in spans]
 
@@ -383,6 +402,7 @@
     self_all,
     neigh_all,
     cb_pad,
+    acts,
     label_rows,
     link_pad,
     logit_own,
@@ -452,8 +472,10 @@
                 )
             )
         started.append(core_copy(ref_of(0, 0), ref_of(0, 1), base + 3))
-        for copy in started:
-            copy.start()
+        for k in (0, 1, 3):
+            started[k].start()
+        yield (0, 0)
+        started[2].start()
         yield (0, 0)
         started[3].wait_recv()
         yield (0, 1)
@@ -483,7 +505,7 @@
 
     def half_route(n, base):
         spans = ((0, 2 * n, n * 96, 48), (1, 2 * n + 1, 192 + n * 96, 48))
-        yield from together(grid_sum(parts, spans, in_wide, in_thin, ssem, rsem, 0, x, y, xs, ys))
+        yield from together(grid_sum(parts, spans, in_wide, in_thin, ssem, rsem, 0, x, y, xs, ys, grid_device))
         at = pl.ds(n * half_rows, half_rows)
         own_self = unpack(parts, x, y, n * 96)
         own_neigh = unpack(parts, x, y, 192 + n * 96) / fan_one
@@ -517,29 +539,27 @@
             *zs,
         )
 
-    used += 48
+    used += 36
     owners = [half_route(n, used + 7 * n) for n in range(2)]
     used += 14
     next(owners[0])
+    next(owners[1])
 
     sent = 160
-    for n in range(4):
-        for a in range(2):
-            for kind in range(2):
-                classes_all[n, a, kind, sent:256, :] = jnp.zeros((256 - sent, hid), jnp.float32)
-    for kind in range(2):
-        classes_all[0, 0, kind, 0:sent, :] = jnp.zeros((sent, hid), jnp.float32)
-    classes_all[0, 0, 0, 0:classes, :] = cs_ref[...].astype(jnp.float32)
-    classes_all[0, 0, 1, 0:classes, :] = cn_ref[...].astype(jnp.float32)
-    class_spread = spread(lambda n, a: classes_all.at[n, a, :, pl.ds(0, sent)], used)
+    classes_all[:, sent:256, :] = jnp.zeros((2, 256 - sent, 8 * hid), jnp.float32)
+    classes_all[:, 0:sent, 0:hid] = jnp.zeros((2, sent, hid), jnp.float32)
+    classes_all[0, 0:classes, 0:hid] = cs_ref[...].astype(jnp.float32)
+    classes_all[1, 0:classes, 0:hid] = cn_ref[...].astype(jnp.float32)
+    class_spread = spread(
+        lambda n, a: classes_all.at[:, pl.ds(0, sent), pl.ds((n * 2 + a) * hid, hid)], used
+    )
     used += 7
+    next(class_spread)
     next(class_spread)
     weights[...] = jnp.zeros_like(weights)
     weights[0:width, :] = ws_ref[...]
     weights[128 : 128 + width, :] = wn_ref[...]
     weights[256 : 256 + width, :] = wn_ref[...]
-    next(owners[0])
-    next(owners[1])
     cb_pad[...] = jnp.zeros_like(cb_pad)
     cb_pad[:, 0:classes] = cb_ref[...]
     extras[...] = jnp.zeros_like(extras)
@@ -556,15 +576,13 @@
     links_b = links_t.astype(jnp.bfloat16)
     target_rows = lax.broadcasted_iota(jnp.int32, (targets, 128), 0)
 
-    def later(route, rounds):
-        for _ in range(rounds):
-            yield
-        yield from route
-
-    run_all(*owners, later(class_spread, 4))
+    run_all(*owners)
 
     pre = pre_parts[z, core] + hb_ref[...]
     piece[0, 0] = pre
+    pre_spread = spread(lambda n, a: piece.at[n, a], used)
+    used += 7
+    next(pre_spread)
     alive = (target_rows < live_ref[0]) & (pre > 0.0)
     hidden = jnp.where(alive, pre, 0.0).astype(jnp.bfloat16)
     hidden_ref[...] = hidden
@@ -572,8 +590,8 @@
     seed_self = active[0:seeds]
     seed_neigh = dot(links_f, hidden) / fan_two
     rows_cols = ((1,), (1,))
-    own_self = high_dot(seed_self, classes_all[0, 0, 0], rows_cols)
-    logit_own[...] = own_self + high_dot(seed_neigh, classes_all[0, 0, 1], rows_cols)
+    own_self = high_dot(seed_self, classes_all[0, :, 0:hid], rows_cols)
+    logit_own[...] = own_self + high_dot(seed_neigh, classes_all[1, :, 0:hid], rows_cols)
     to_core = core_copy(logit_own, logit_core, used)
     used += 1
     to_core.start()
@@ -598,12 +616,11 @@
 
     sends = z_sends(logit_z.at[z], used)
     used += 3
-    pre_spread = spread(lambda n, a: piece.at[n, a], used)
-    used += 7
     next(pre_spread)
+    run_all(class_spread)
     self_t = self_all[...].T[0:width].astype(jnp.bfloat16)
     neigh_t_hi, neigh_t_lo = split(neigh_all[...].T[0:width])
-    rows_hi = jnp.concatenate([self_t, neigh_t_hi], axis=0)
+    rows_three = jnp.concatenate([self_t, neigh_t_hi, neigh_t_lo], axis=0)
     for c in sends:
         c.wait()
     logits = (logit_z[0] + logit_z[1]) + (logit_z[2] + logit_z[3]) + cb_pad[...]
@@ -614,19 +631,23 @@
     onehot = jnp.where(lanes == label_rows[...], 1.0, 0.0)
     losses = log_total - jnp.sum(onehot * logits, axis=1, keepdims=True)
     dlogit = jnp.exp(logits - log_total) - onehot
-    dlogit_hi, dlogit_lo = split(dlogit)
-
-    def back(n, across, kind):
-        side = classes_all[n, across, kind].astype(jnp.bfloat16)
-        return dot(dlogit_hi, side) + dot(dlogit_lo, side)
+    dlogit_two = jnp.concatenate(split(dlogit), axis=0)
+
+    def back(kind):
+        both = dot(dlogit_two, classes_all[kind].astype(jnp.bfloat16))
+        return both[0:seeds] + both[seeds : 2 * seeds]
+
+    back_neigh = jnp.concatenate(
+        [back(1) / fan_two, jnp.zeros((128 - seeds, 8 * hid), jnp.float32)], axis=0
+    )
+    links_two = jnp.concatenate([links_b, links_b], axis=1)
+    acts[...] = dot(links_two, jnp.concatenate(split(back_neigh), axis=0))
+    acts[0:seeds, :] = acts[0:seeds, :] + back(0)
+    live_rows = target_rows < live_ref[0]
 
     def grad_of(n, across):
-        low = jnp.zeros((128 - seeds, hid), jnp.float32)
-        neigh_hi, neigh_lo = split(jnp.concatenate([back(n, across, 1) / fan_two, low], axis=0))
-        top_rows = jnp.concatenate([back(n, across, 0), jnp.zeros((targets - seeds, hid), jnp.float32)], axis=0)
-        act = dot(links_b, neigh_hi) + dot(links_b, neigh_lo) + top_rows
-        on = (target_rows < live_ref[0]) & (piece[n, across] > 0.0)
-        return jnp.where(on, act, 0.0)
+        at = (n * 2 + across) * hid
+        return jnp.where(live_rows & (piece[n, across] > 0.0), acts[:, at : at + hid], 0.0)
 
     term_base = used
     used += groups
@@ -651,10 +672,10 @@
         grad_pre = grad_of(n, across)
         if step == 0:
             hidden_line.append(jnp.sum(grad_pre, axis=0, keepdims=True))
-        g_hi, g_lo = split(grad_pre)
-        term = dot(rows_hi, g_hi) + dot(rows_hi, g_lo)
-        terms[2 * step] = term[0:width]
-        terms[2 * step + 1] = term[width : 2 * width] + dot(neigh_t_lo, g_hi)
+        term = dot(rows_three, jnp.concatenate(split(grad_pre), axis=1))
+        terms[2 * step] = term[0:width, 0:hid] + term[0:width, hid : 2 * hid]
+        neigh_term = term[width : 2 * width, 0:hid] + term[width : 2 * width, hid : 2 * hid]
+        terms[2 * step + 1] = neigh_term + term[2 * width : 3 * width, 0:hid]
         for s in range(2):
             k = 2 * step + s
             dests[k] = dest = zz * 4 + cc * 2 + s
@@ -797,15 +818,16 @@
     shapes = [
         ((4, 4, 384, 128), f32),
         ((4, 6, 4, 48, 128), f32),
-        ((4, 6, 48, 128), f32),
+        ((4, 3, 96, 128), f32),
         ((384, hidden_all), jnp.bfloat16),
         ((4, 2, targets, hid), f32),
         ((4, targets, hid), f32),
         ((2, 6, targets // 4, hid), f32),
-        ((4, 2, 2, 256, hid), f32),
+        ((2, 256, 8 * hid), f32),
         ((targets, 128), f32),
         ((targets, 128), f32),
         ((1, 256), f32),
+        ((targets, 8 * hid), f32),
         ((seeds, 256), jnp.int32),
         ((targets, 128), f32),
         ((seeds, 256), f32),

time: 119 us -> 114 us (0.958)
  Pallas kernels: 114 us -> 109 us
    pallas_call x1, Pallas kernels: 81.6 us -> 76.7 us  [body(): pl.pallas_call(functools.partial(exchange_kernel, fan_one, fan_two), out_...]
where the time goes in v4:
time: 114 us
  Pallas kernels  109 us (96%)
  local copies, waits for them, and re-layouts  3.29 us (3%)
  between operations  1.42 us (1%)
    pallas_call x1, Pallas kernels, body(): pl.pallas_call(functools.partial(exchange_kernel, fan_one, fan_two), out_...  76.7 us
    pallas_call x1, Pallas kernels, gather_rows(): pl.pallas_call(gather_kernel, out_shape=jax.ShapeDtypeStruct((batches, 38...  30 us
    unnamed x24, local copies, waits for them, and re-layouts  3.29 us

profile of v4, /device:TPU:0, one launch (start us, length us, event | category | flops | bytes accessed | tf_op | source)
XLA Modules:
  0.0 113.7 jit_solution(702737798313558552)
XLA Ops:
  1.3 0.0 copy-start.1
  1.3 1.0 copy-done.1
  2.3 0.0 copy-start.7
  2.3 0.7 copy-done.7
  3.0 0.0 copy-start.2
  3.0 0.0 copy-start.3
  3.0 0.0 copy-start.8
  3.0 0.0 copy-start.9
  3.0 0.0 copy-start.10
  3.0 0.0 copy-start.11
  3.1 30.0 %gather_rows.1 = f32[16,384,128]{2,1,0:T(8,128)S(1)} custom-call(s32[1]{0:T(128)} %bitcast.offset_ref, bf16[96,16384]{1,0:T(8,128)(2,1)} %feat_hbm.1, s32[16,256]{1,0:T(8,128)S(1)} %copy-done.7, s32[25,16,256]{2,1,0:T(8,128)S(1)} %bitcast.17), custom_call_target="tpu_custom_call" | custom-call | tf_op jit(solution)/shard_map/gather_rows/pallas_call | solution.py:183
  33.1 0.0 copy-done.2
  33.1 0.0 copy-done.3
  33.1 0.0 copy-done.5
  33.1 0.0 copy-done.6
  33.1 0.0 copy-done.8
  33.1 0.0 copy-done.9
  33.1 0.0 copy-done.10
  33.1 0.0 copy-done.11
  33.1 76.7 %exchange.1 = (bf16[256,128]{1,0:T(8,128)(2,1)S(1)}, f32[4,4,120,128]{3,2,1,0:T(8,128)S(1)}) custom-call(f32[4,4,384,128]{3,2,1,0:T(8,128)S(1)} %bitcast.15, bf16[96,1024]{1,0:T(8,128)(2,1)S(1)} %copy-done.2, bf16[96,1024]{1,0:T(8,128)(2,1)S(1)} %copy-done.3, f32[1,128]{1,0:T(1,128)S(1)} %bitcast.22, bf16[153,128]{1,0:T(8,128)(2,1)S(1)} %bitcast.18, ...), custom_call_target="tpu_custom_call" | custom-call | tf_op jit(solution)/shard_map/exchange/pallas_call | solution.py:842
  109.9 0.0 copy-start
  109.9 0.9 copy-done
  110.8 0.6 copy-done.4
  111.4 2.2 %finish.1 = (bf16[256,128]{1,0:T(8,128)(2,1)}, f32[96,1024]{1,0:T(8,128)}, f32[96,1024]{1,0:T(8,128)}, f32[1,128]{1,0:T(1,128)}, f32[153,128]{1,0:T(8,128)}, /*i...) custom-call(bf16[256,128]{1,0:T(8,128)(2,1)} %copy-done.4, f32[16,120,128]{2,1,0:T(8,128)} %bitcast.16), custom_call_target="tpu_custom_call" | custom-call | tf_op jit(solution)/shard_map/finish/pallas_call | solution.py:872
  (3 shorter events, 0.0 us)
Async XLA Ops:
  1.3 1.0 copy-start.1
  2.3 0.7 copy-start.7
  3.0 30.1 %copy-start.2 = (bf16[96,1024]{1,0:T(8,128)(2,1)S(1)}, bf16[96,1024]{1,0:T(8,128)(2,1)}, u32[]{:S(2)}) copy-start(bf16[96,1024]{1,0:T(8,128)(2,1)} %ws_ref.1) | copy-start | bytes 589828
  3.0 30.1 %copy-start.3 = (bf16[96,1024]{1,0:T(8,128)(2,1)S(1)}, bf16[96,1024]{1,0:T(8,128)(2,1)}, u32[]{:S(2)}) copy-start(bf16[96,1024]{1,0:T(8,128)(2,1)} %wn_ref.1) | copy-start | bytes 589828
  3.0 30.1 %copy-start.5 = (bf16[128,153]{0,1:T(8,128)(2,1)S(1)}, bf16[128,153]{0,1:T(8,128)(2,1)}, u32[]{:S(2)}) copy-start(bf16[128,153]{0,1:T(8,128)(2,1)} %param.21) | copy-start | bytes 117508
  3.0 30.1 %copy-start.6 = (bf16[128,153]{0,1:T(8,128)(2,1)S(1)}, bf16[128,153]{0,1:T(8,128)(2,1)}, u32[]{:S(2)}) copy-start(bf16[128,153]{0,1:T(8,128)(2,1)} %param.22) | copy-start | bytes 117508
  3.0 30.1 %copy-start.8 = (s32[1,32,15]{1,0,2:T(1,128)S(1)}, s32[1,32,15]{1,0,2:T(1,128)}, u32[]{:S(2)}) copy-start(s32[1,32,15]{1,0,2:T(1,128)} %param.16) | copy-start | bytes 5764
  3.0 30.1 %copy-start.9 = (f32[153]{0:T(256)S(1)}, f32[153]{0:T(256)}, u32[]{:S(2)}) copy-start(f32[153]{0:T(256)} %param.23) | copy-start | bytes 1840
  3.0 30.1 %copy-start.10 = (f32[128]{0:T(128)S(1)}, f32[128]{0:T(128)}, u32[]{:S(2)}) copy-start(f32[128]{0:T(128)} %param.20) | copy-start | bytes 1540
  3.0 30.1 %copy-start.11 = (s32[1,32]{1,0:T(1,128)S(1)}, s32[1,32]{1,0:T(1,128)}, u32[]{:S(2)}) copy-start(s32[1,32]{1,0:T(1,128)} %labels_ref.1) | copy-start | bytes 388
  109.9 0.9 copy-start
  110.8 0.6 copy-start.4

commit v5 on v4

--- a/solution.py
+++ b/solution.py
@@ -8,8 +8,8 @@
 
 UNROLL = 16
 TOP = 3
-BLOCK = 4
-TURNS = 18
+BLOCK = 14
+TURNS = 64
 
 
 def gather_kernel(offset_ref, feat_hbm, targets_hbm, hops_hbm, out_ref, feat_ref, targets_ref, hops_ref, table, acc, ids, codes, counts, first_s, counts_s, extra_s, sems, load_sems):
@@ -528,16 +528,25 @@
         copy.wait()
         for zz in range(4):
             pre_parts[zz, core, at] = pre_parts[zz, core, at] + in_core[zz, at]
-        quarter = half_rows // 2
-        yield from ring_sum(
-            lambda d, p: pre_parts.at[d, core, pl.ds(n * half_rows + p * quarter, quarter)],
-            lambda k: in_z.at[n, k],
-            ssem,
-            rsem,
-            base + 1,
-            z,
-            *zs,
-        )
+        copies = []
+        for k, (step, near) in enumerate(((1, zs[0]), (3, zs[1]), (2, opposite))):
+            copies.append(
+                pltpu.make_async_remote_copy(
+                    src_ref=pre_parts.at[lax.rem(z + step, 4), core, at],
+                    dst_ref=in_z.at[n, k],
+                    send_sem=ssem.at[base + 1 + k],
+                    recv_sem=rsem.at[base + 1 + k],
+                    device_id=near,
+                    device_id_type=MESH,
+                )
+            )
+            copies[-1].start()
+        yield
+        for k, copy in enumerate(copies):
+            copy.wait_recv()
+            pre_parts[z, core, at] = pre_parts[z, core, at] + in_z[n, k]
+        for copy in copies:
+            copy.wait_send()
 
     used += 36
     owners = [half_route(n, used + 7 * n) for n in range(2)]
@@ -822,7 +831,7 @@
         ((384, hidden_all), jnp.bfloat16),
         ((4, 2, targets, hid), f32),
         ((4, targets, hid), f32),
-        ((2, 6, targets // 4, hid), f32),
+        ((2, 3, targets // 2, hid), f32),
         ((2, 256, 8 * hid), f32),
         ((targets, 128), f32),
         ((targets, 128), f32),
@@ -884,6 +893,7 @@
         in_specs=[vmem] * 2,
         out_specs=(vmem,) * 8,
         scratch_shapes=[pltpu.VMEM((16 * 24, 128), f32)],
+        compiler_params=pltpu.CompilerParams(vmem_limit_bytes=8 * 1024 * 1024),
         name="finish",
     )(hidden_layer, sums.reshape(16, width + 24, 128))
     return (

time: 114 us -> 106 us (0.930)
  Pallas kernels: 109 us -> 102 us
  local copies, waits for them, and re-layouts: 3.29 us -> 1.74 us
    pallas_call x1, Pallas kernels: 30 us -> 27.2 us  [gather_rows(): pl.pallas_call(gather_kernel, out_shape=jax.ShapeDtypeStruct((batches, 38...]
    pallas_call x1, Pallas kernels: 76.7 us -> 74 us  [body(): pl.pallas_call(functools.partial(exchange_kernel, fan_one, fan_two), out_...]
    unnamed x24 -> x20, local copies, waits for them, and re-layouts: 3.29 us -> 1.74 us
    pallas_call x1, Pallas kernels: 2.23 us -> 0.99 us  [body(): pl.pallas_call(functools.partial(finish_kernel, 1.0 / (batches * seeds)),...]
where the time goes in v5:
time: 106 us; the launch traced here: 105 us
  Pallas kernels  102 us (96%)
  local copies, waits for them, and re-layouts  1.74 us (2%)
  between operations  1.41 us (1%)
    pallas_call x1, Pallas kernels, body(): pl.pallas_call(functools.partial(exchange_kernel, fan_one, fan_two), out_...  74 us
    pallas_call x1, Pallas kernels, gather_rows(): pl.pallas_call(gather_kernel, out_shape=jax.ShapeDtypeStruct((batches, 38...  27.2 us

profile of v5, /device:TPU:0, one launch (start us, length us, event | category | flops | bytes accessed | tf_op | source)
XLA Modules:
  0.0 105.4 jit_solution(11277979981921139253)
XLA Ops:
  1.3 0.0 copy-start
  1.3 1.0 copy-done
  2.3 0.0 copy-start.5
  2.3 0.7 copy-done.5
  3.0 0.0 copy-start.1
  3.0 0.0 copy-start.2
  3.0 0.0 copy-start.3
  3.0 0.0 copy-start.4
  3.0 0.0 copy-start.6
  3.0 0.0 copy-start.7
  3.0 0.0 copy-start.8
  3.0 0.0 copy-start.9
  3.1 27.2 %gather_rows.1 = f32[16,384,128]{2,1,0:T(8,128)S(1)} custom-call(s32[1]{0:T(128)} %bitcast.offset_ref, bf16[96,16384]{1,0:T(8,128)(2,1)} %feat_hbm.1, s32[16,256]{1,0:T(8,128)S(1)} %copy-done.5, s32[25,16,256]{2,1,0:T(8,128)S(1)} %bitcast.17), custom_call_target="tpu_custom_call" | custom-call | tf_op jit(solution)/shard_map/gather_rows/pallas_call | solution.py:183
  30.2 0.0 copy-done.1
  30.2 0.0 copy-done.2
  30.3 0.0 copy-done.3
  30.3 0.0 copy-done.4
  30.3 0.0 copy-done.6
  30.3 0.0 copy-done.7
  30.3 0.0 copy-done.8
  30.3 0.0 copy-done.9
  30.3 74.0 %exchange.1 = (bf16[256,128]{1,0:T(8,128)(2,1)S(1)}, f32[4,4,120,128]{3,2,1,0:T(8,128)S(1)}) custom-call(f32[4,4,384,128]{3,2,1,0:T(8,128)S(1)} %bitcast.15, bf16[96,1024]{1,0:T(8,128)(2,1)S(1)} %copy-done.1, bf16[96,1024]{1,0:T(8,128)(2,1)S(1)} %copy-done.2, f32[1,128]{1,0:T(1,128)S(1)} %bitcast.22, bf16[153,128]{1,0:T(8,128)(2,1)S(1)} %bitcast.18, ...), custom_call_target="tpu_custom_call" | custom-call | tf_op jit(solution)/shard_map/exchange/pallas_call | solution.py:851
  104.4 1.0 finish.1
Async XLA Ops:
  1.3 1.0 copy-start
  2.3 0.7 copy-start.5
  3.0 27.2 %copy-start.1 = (bf16[96,1024]{1,0:T(8,128)(2,1)S(1)}, bf16[96,1024]{1,0:T(8,128)(2,1)}, u32[]{:S(2)}) copy-start(bf16[96,1024]{1,0:T(8,128)(2,1)} %ws_ref.1) | copy-start | bytes 589828
  3.0 27.2 %copy-start.2 = (bf16[96,1024]{1,0:T(8,128)(2,1)S(1)}, bf16[96,1024]{1,0:T(8,128)(2,1)}, u32[]{:S(2)}) copy-start(bf16[96,1024]{1,0:T(8,128)(2,1)} %wn_ref.1) | copy-start | bytes 589828
  3.0 27.2 %copy-start.3 = (bf16[128,153]{0,1:T(8,128)(2,1)S(1)}, bf16[128,153]{0,1:T(8,128)(2,1)}, u32[]{:S(2)}) copy-start(bf16[128,153]{0,1:T(8,128)(2,1)} %param.21) | copy-start | bytes 117508
  3.0 27.3 %copy-start.4 = (bf16[128,153]{0,1:T(8,128)(2,1)S(1)}, bf16[128,153]{0,1:T(8,128)(2,1)}, u32[]{:S(2)}) copy-start(bf16[128,153]{0,1:T(8,128)(2,1)} %param.22) | copy-start | bytes 117508
  3.0 27.3 %copy-start.6 = (s32[1,32,15]{1,0,2:T(1,128)S(1)}, s32[1,32,15]{1,0,2:T(1,128)}, u32[]{:S(2)}) copy-start(s32[1,32,15]{1,0,2:T(1,128)} %param.16) | copy-start | bytes 5764
  3.0 27.3 %copy-start.7 = (f32[153]{0:T(256)S(1)}, f32[153]{0:T(256)}, u32[]{:S(2)}) copy-start(f32[153]{0:T(256)} %param.23) | copy-start | bytes 1840
  3.0 27.3 %copy-start.8 = (f32[128]{0:T(128)S(1)}, f32[128]{0:T(128)}, u32[]{:S(2)}) copy-start(f32[128]{0:T(128)} %param.20) | copy-start | bytes 1540
  3.0 27.3 %copy-start.9 = (s32[1,32]{1,0:T(1,128)S(1)}, s32[1,32]{1,0:T(1,128)}, u32[]{:S(2)}) copy-start(s32[1,32]{1,0:T(1,128)} %labels_ref.1) | copy-start | bytes 388

commit v6 on v5

--- a/solution.py
+++ b/solution.py
@@ -206,7 +206,6 @@
 
 
 MESH = pl.DeviceIdType.MESH
-HIGH = lax.Precision.HIGHEST
 
 
 def run_all(*routes):
@@ -372,10 +371,6 @@
     return jnp.dot(a, b, preferred_element_type=jnp.float32)
 
 
-def high_dot(a, b, dims=((1,), (0,))):
-    return lax.dot_general(a, b, (dims, ((), ())), precision=HIGH, preferred_element_type=jnp.float32)
-
-
 def exchange_kernel(
     fan_one,
     fan_two,
@@ -399,6 +394,8 @@
     in_core,
     in_z,
     classes_all,
+    class_low,
+    class_three,
     self_all,
     neigh_all,
     cb_pad,
@@ -442,7 +439,8 @@
     load = pltpu.make_async_copy(parts_ref, parts, local_sem)
     load.start()
     barrier = pltpu.get_barrier_semaphore()
-    nears = others + list(zs) + [opposite, sibling]
+    axis_far = [grid_device(2, 0), grid_device(0, 2)]
+    nears = list(xs + ys + zs) + axis_far + [opposite, sibling]
     for near in nears:
         pl.semaphore_signal(barrier, inc=1, device_id=near, device_id_type=MESH)
     pl.semaphore_wait(barrier, len(nears))
@@ -585,6 +583,8 @@
     links_b = links_t.astype(jnp.bfloat16)
     target_rows = lax.broadcasted_iota(jnp.int32, (targets, 128), 0)
 
+    own_classes = [classes_all[kind, :, 0:hid].astype(jnp.bfloat16) for kind in range(2)]
+    class_three[...] = jnp.concatenate([own_classes[0], own_classes[1], own_classes[1]], axis=1)
     run_all(*owners)
 
     pre = pre_parts[z, core] + hb_ref[...]
@@ -595,12 +595,12 @@
     alive = (target_rows < live_ref[0]) & (pre > 0.0)
     hidden = jnp.where(alive, pre, 0.0).astype(jnp.bfloat16)
     hidden_ref[...] = hidden
-    active = hidden.astype(jnp.float32)
-    seed_self = active[0:seeds]
     seed_neigh = dot(links_f, hidden) / fan_two
-    rows_cols = ((1,), (1,))
-    own_self = high_dot(seed_self, classes_all[0, :, 0:hid], rows_cols)
-    logit_own[...] = own_self + high_dot(seed_neigh, classes_all[1, :, 0:hid], rows_cols)
+    neigh_two = jnp.concatenate(split(seed_neigh), axis=1)
+    seed_three = jnp.concatenate([hidden[0:seeds], neigh_two], axis=1)
+    logit_own[...] = lax.dot_general(
+        seed_three, class_three[...], (((1,), (1,)), ((), ())), preferred_element_type=jnp.float32
+    )
     to_core = core_copy(logit_own, logit_core, used)
     used += 1
     to_core.start()
@@ -627,6 +627,8 @@
     used += 3
     next(pre_spread)
     run_all(class_spread)
+    for kind in range(2):
+        class_low[kind] = classes_all[kind].astype(jnp.bfloat16)
     self_t = self_all[...].T[0:width].astype(jnp.bfloat16)
     neigh_t_hi, neigh_t_lo = split(neigh_all[...].T[0:width])
     rows_three = jnp.concatenate([self_t, neigh_t_hi, neigh_t_lo], axis=0)
@@ -643,7 +645,7 @@
     dlogit_two = jnp.concatenate(split(dlogit), axis=0)
 
     def back(kind):
-        both = dot(dlogit_two, classes_all[kind].astype(jnp.bfloat16))
+        both = dot(dlogit_two, class_low[kind])
         return both[0:seeds] + both[seeds : 2 * seeds]
 
     back_neigh = jnp.concatenate(
@@ -700,9 +702,11 @@
     block_terms(0, 0, 0)
     block_terms(1, *next(pre_spread))
 
-    dlogit_t = dlogit.T[0:sent]
+    dlogit_t = jnp.concatenate(split(dlogit.T[0:sent]), axis=0)
+    both = dot(dlogit_t, seed_three)
+    both = [both[:, n * hid : n * hid + hid] for n in range(3)]
     class_grads = jnp.concatenate(
-        [high_dot(dlogit_t, seed_self), high_dot(dlogit_t, seed_neigh)], axis=0
+        [both[0][0:sent] + both[0][sent:], both[1][0:sent] + both[1][sent:] + both[2][0:sent]], axis=0
     )
     per = extras.shape[1]
     for n in range(0, 320, 8):
@@ -833,6 +837,8 @@
         ((4, targets, hid), f32),
         ((2, 3, targets // 2, hid), f32),
         ((2, 256, 8 * hid), f32),
+        ((2, 256, 8 * hid), jnp.bfloat16),
+        ((256, 3 * hid), jnp.bfloat16),
         ((targets, 128), f32),
         ((targets, 128), f32),
         ((1, 256), f32),

time: 106 us -> 104 us (0.981)
    pallas_call x1, Pallas kernels: 74 us -> 72.7 us  [body(): pl.pallas_call(functools.partial(exchange_kernel, fan_one, fan_two), out_...]
where the time goes in v6:
time: 104 us
  Pallas kernels  101 us (97%)
  local copies, waits for them, and re-layouts  1.74 us (2%)
  between operations  1.41 us (1%)
    pallas_call x1, Pallas kernels, body(): pl.pallas_call(functools.partial(exchange_kernel, fan_one, fan_two), out_...  72.7 us
    pallas_call x1, Pallas kernels, gather_rows(): pl.pallas_call(gather_kernel, out_shape=jax.ShapeDtypeStruct((batches, 38...  27.2 us

profile of v6, /device:TPU:0, one launch (start us, length us, event | category | flops | bytes accessed | tf_op | source)
XLA Modules:
  0.0 104.1 jit_solution(12027214654925855500)
XLA Ops:
  1.3 0.0 copy-start
  1.3 1.0 copy-done
  2.3 0.0 copy-start.5
  2.3 0.7 copy-done.5
  3.0 0.0 copy-start.1
  3.0 0.0 copy-start.2
  3.0 0.0 copy-start.3
  3.0 0.0 copy-start.4
  3.0 0.0 copy-start.6
  3.0 0.0 copy-start.7
  3.0 0.0 copy-start.8
  3.0 0.0 copy-start.9
  3.1 27.2 %gather_rows.1 = f32[16,384,128]{2,1,0:T(8,128)S(1)} custom-call(s32[1]{0:T(128)} %bitcast.offset_ref, bf16[96,16384]{1,0:T(8,128)(2,1)} %feat_hbm.1, s32[16,256]{1,0:T(8,128)S(1)} %copy-done.5, s32[25,16,256]{2,1,0:T(8,128)S(1)} %bitcast.17), custom_call_target="tpu_custom_call" | custom-call | tf_op jit(solution)/shard_map/gather_rows/pallas_call | solution.py:183
  30.3 0.0 copy-done.1
  30.3 0.0 copy-done.2
  30.3 0.0 copy-done.3
  30.3 0.0 copy-done.4
  30.3 0.0 copy-done.6
  30.3 0.0 copy-done.7
  30.3 0.0 copy-done.8
  30.3 0.0 copy-done.9
  30.4 72.7 %exchange.1 = (bf16[256,128]{1,0:T(8,128)(2,1)S(1)}, f32[4,4,120,128]{3,2,1,0:T(8,128)S(1)}) custom-call(f32[4,4,384,128]{3,2,1,0:T(8,128)S(1)} %bitcast.15, bf16[96,1024]{1,0:T(8,128)(2,1)S(1)} %copy-done.1, bf16[96,1024]{1,0:T(8,128)(2,1)S(1)} %copy-done.2, f32[1,128]{1,0:T(1,128)S(1)} %bitcast.22, bf16[153,128]{1,0:T(8,128)(2,1)S(1)} %bitcast.18, ...), custom_call_target="tpu_custom_call" | custom-call | tf_op jit(solution)/shard_map/exchange/pallas_call | solution.py:857
  103.1 1.0 finish.1
Async XLA Ops:
  1.3 1.0 copy-start
  2.3 0.7 copy-start.5
  3.0 27.3 %copy-start.1 = (bf16[96,1024]{1,0:T(8,128)(2,1)S(1)}, bf16[96,1024]{1,0:T(8,128)(2,1)}, u32[]{:S(2)}) copy-start(bf16[96,1024]{1,0:T(8,128)(2,1)} %ws_ref.1) | copy-start | bytes 589828
  3.0 27.3 %copy-start.2 = (bf16[96,1024]{1,0:T(8,128)(2,1)S(1)}, bf16[96,1024]{1,0:T(8,128)(2,1)}, u32[]{:S(2)}) copy-start(bf16[96,1024]{1,0:T(8,128)(2,1)} %wn_ref.1) | copy-start | bytes 589828
  3.0 27.3 %copy-start.3 = (bf16[128,153]{0,1:T(8,128)(2,1)S(1)}, bf16[128,153]{0,1:T(8,128)(2,1)}, u32[]{:S(2)}) copy-start(bf16[128,153]{0,1:T(8,128)(2,1)} %param.21) | copy-start | bytes 117508
  3.0 27.3 %copy-start.4 = (bf16[128,153]{0,1:T(8,128)(2,1)S(1)}, bf16[128,153]{0,1:T(8,128)(2,1)}, u32[]{:S(2)}) copy-start(bf16[128,153]{0,1:T(8,128)(2,1)} %param.22) | copy-start | bytes 117508
  3.0 27.3 %copy-start.6 = (s32[1,32,15]{1,0,2:T(1,128)S(1)}, s32[1,32,15]{1,0,2:T(1,128)}, u32[]{:S(2)}) copy-start(s32[1,32,15]{1,0,2:T(1,128)} %param.16) | copy-start | bytes 5764
  3.0 27.3 %copy-start.7 = (f32[153]{0:T(256)S(1)}, f32[153]{0:T(256)}, u32[]{:S(2)}) copy-start(f32[153]{0:T(256)} %param.23) | copy-start | bytes 1840
  3.0 27.3 %copy-start.8 = (f32[128]{0:T(128)S(1)}, f32[128]{0:T(128)}, u32[]{:S(2)}) copy-start(f32[128]{0:T(128)} %param.20) | copy-start | bytes 1540
  3.0 27.3 %copy-start.9 = (s32[1,32]{1,0:T(1,128)S(1)}, s32[1,32]{1,0:T(1,128)}, u32[]{:S(2)}) copy-start(s32[1,32]{1,0:T(1,128)} %labels_ref.1) | copy-start | bytes 388

commit v7 on v6

--- a/solution.py
+++ b/solution.py
@@ -8,8 +8,8 @@
 
 UNROLL = 16
 TOP = 3
-BLOCK = 14
-TURNS = 64
+BLOCK = 28
+TURNS = 128
 
 
 def gather_kernel(offset_ref, feat_hbm, targets_hbm, hops_hbm, out_ref, feat_ref, targets_ref, hops_ref, table, acc, ids, codes, counts, first_s, counts_s, extra_s, sems, load_sems):

time: 104 us -> 104 us (level)
  no operation moved by 1% of the time
where the time goes in v7:
time: 104 us; the launch traced here: 103 us
  Pallas kernels  100 us (96%)
  local copies, waits for them, and re-layouts  1.74 us (2%)
  between operations  1.41 us (1%)
    pallas_call x1, Pallas kernels, body(): pl.pallas_call(functools.partial(exchange_kernel, fan_one, fan_two), out_...  72.6 us
    pallas_call x1, Pallas kernels, gather_rows(): pl.pallas_call(gather_kernel, out_shape=jax.ShapeDtypeStruct((batches, 38...  26.4 us

profile of v7, /device:TPU:0, one launch (start us, length us, event | category | flops | bytes accessed | tf_op | source)
XLA Modules:
  0.0 103.1 jit_solution(12715506571324670293)
XLA Ops:
  1.3 0.0 copy-start
  1.3 1.0 copy-done
  2.3 0.0 copy-start.5
  2.3 0.7 copy-done.5
  3.0 0.0 copy-start.1
  3.0 0.0 copy-start.2
  3.0 0.0 copy-start.3
  3.0 0.0 copy-start.4
  3.0 0.0 copy-start.6
  3.0 0.0 copy-start.7
  3.0 0.0 copy-start.8
  3.0 0.0 copy-start.9
  3.1 26.4 %gather_rows.1 = f32[16,384,128]{2,1,0:T(8,128)S(1)} custom-call(s32[1]{0:T(128)} %bitcast.offset_ref, bf16[96,16384]{1,0:T(8,128)(2,1)} %feat_hbm.1, s32[16,256]{1,0:T(8,128)S(1)} %copy-done.5, s32[25,16,256]{2,1,0:T(8,128)S(1)} %bitcast.17), custom_call_target="tpu_custom_call" | custom-call | tf_op jit(solution)/shard_map/gather_rows/pallas_call | solution.py:183
  29.4 0.0 copy-done.1
  29.4 0.0 copy-done.2
  29.4 0.0 copy-done.3
  29.4 0.0 copy-done.4
  29.5 0.0 copy-done.6
  29.5 0.0 copy-done.7
  29.5 0.0 copy-done.8
  29.5 0.0 copy-done.9
  29.5 72.6 %exchange.1 = (bf16[256,128]{1,0:T(8,128)(2,1)S(1)}, f32[4,4,120,128]{3,2,1,0:T(8,128)S(1)}) custom-call(f32[4,4,384,128]{3,2,1,0:T(8,128)S(1)} %bitcast.15, bf16[96,1024]{1,0:T(8,128)(2,1)S(1)} %copy-done.1, bf16[96,1024]{1,0:T(8,128)(2,1)S(1)} %copy-done.2, f32[1,128]{1,0:T(1,128)S(1)} %bitcast.22, bf16[153,128]{1,0:T(8,128)(2,1)S(1)} %bitcast.18, ...), custom_call_target="tpu_custom_call" | custom-call | tf_op jit(solution)/shard_map/exchange/pallas_call | solution.py:857
  102.1 1.0 finish.1
Async XLA Ops:
  1.3 1.0 copy-start
  2.3 0.7 copy-start.5
  3.0 26.4 %copy-start.1 = (bf16[96,1024]{1,0:T(8,128)(2,1)S(1)}, bf16[96,1024]{1,0:T(8,128)(2,1)}, u32[]{:S(2)}) copy-start(bf16[96,1024]{1,0:T(8,128)(2,1)} %ws_ref.1) | copy-start | bytes 589828
  3.0 26.4 %copy-start.2 = (bf16[96,1024]{1,0:T(8,128)(2,1)S(1)}, bf16[96,1024]{1,0:T(8,128)(2,1)}, u32[]{:S(2)}) copy-start(bf16[96,1024]{1,0:T(8,128)(2,1)} %wn_ref.1) | copy-start | bytes 589828
  3.0 26.4 %copy-start.3 = (bf16[128,153]{0,1:T(8,128)(2,1)S(1)}, bf16[128,153]{0,1:T(8,128)(2,1)}, u32[]{:S(2)}) copy-start(bf16[128,153]{0,1:T(8,128)(2,1)} %param.21) | copy-start | bytes 117508
  3.0 26.4 %copy-start.4 = (bf16[128,153]{0,1:T(8,128)(2,1)S(1)}, bf16[128,153]{0,1:T(8,128)(2,1)}, u32[]{:S(2)}) copy-start(bf16[128,153]{0,1:T(8,128)(2,1)} %param.22) | copy-start | bytes 117508
  3.0 26.4 %copy-start.6 = (s32[1,32,15]{1,0,2:T(1,128)S(1)}, s32[1,32,15]{1,0,2:T(1,128)}, u32[]{:S(2)}) copy-start(s32[1,32,15]{1,0,2:T(1,128)} %param.16) | copy-start | bytes 5764
  3.0 26.4 %copy-start.7 = (f32[153]{0:T(256)S(1)}, f32[153]{0:T(256)}, u32[]{:S(2)}) copy-start(f32[153]{0:T(256)} %param.23) | copy-start | bytes 1840
  3.0 26.4 %copy-start.8 = (f32[128]{0:T(128)S(1)}, f32[128]{0:T(128)}, u32[]{:S(2)}) copy-start(f32[128]{0:T(128)} %param.20) | copy-start | bytes 1540
  3.0 26.4 %copy-start.9 = (s32[1,32]{1,0:T(1,128)S(1)}, s32[1,32]{1,0:T(1,128)}, u32[]{:S(2)}) copy-start(s32[1,32]{1,0:T(1,128)} %labels_ref.1) | copy-start | bytes 388
